TPU v7x, 32 devices: a whole 2x2x4 slice. The times are simulated.
32 devices in a mesh: gx: 16 (over z, x, core), gy: 2 (over y).
Axes of the slice: x: 2, y: 2, z: 4, core: 2. Of those that a mesh axis runs over, the one named last changes fastest.
Arguments:
- positions: float32 [3, 16, 4, 12, 128], P(None, 'gx', 'gy'), may hold values from 0 to 1
- velocities: float32 [3, 16, 4, 12, 128], P(None, 'gx', 'gy'), may hold values from -8 to 8
- counts: int32 [16, 4, 12], P('gx', 'gy'), may hold values from 64 to 128
Outputs:
- positions_out: float32 [3, 16, 4, 12, 128], P(None, 'gx', 'gy')
- velocities_out: float32 [3, 16, 4, 12, 128], P(None, 'gx', 'gy')
- forces_out: float32 [3, 16, 4, 12, 128], P(None, 'gx', 'gy')
Inputs may be any that keep to these rules, and one draw needn't show every extreme that they name: `counts`: the number of atoms in a cell; slots from that number up to 128 are empty.
All inputs are finite; a program needn't handle non-finite values.
Results may differ from a plain program's by a relative error of at most 0.0001.
Values sent between devices are 32-bit elements; how exact they have to be, the bound alone decides.
A program may use at most 64 MiB of HBM per device.

v0:
```python
import jax
import jax.numpy as jnp
from jax import lax
from jax.sharding import PartitionSpec as P

STEPS = 2


TIME_STEP = 0.05
DENSITY_SCALE = 0.0625
PAIR_SCALE = 0.0625


def passed_along(block, axis, distance):
    devices = range(lax.axis_size(axis))
    route = [((i - distance) % len(devices), i) for i in devices]
    return lax.ppermute(block, axis, route)


def with_halo(value, sides, width):
    for axis, dim in sides:
        devices, length = (lax.axis_size(axis), value.shape[dim])
        up = [(i, (i + 1) % devices) for i in range(devices)]
        down = [(j, i) for i, j in up]
        last = lax.slice_in_dim(value, length - width, length, axis=dim)
        first = lax.slice_in_dim(value, 0, width, axis=dim)
        before = lax.ppermute(last, axis, up)
        after = lax.ppermute(first, axis, down)
        value = jnp.concatenate([before, value, after], axis=dim)
    return value


def slots_filled(amount, slots):
    places = lax.broadcasted_iota(amount.dtype, amount.shape + (slots,), amount.ndim)
    return (places < amount[..., None]).astype(amount.dtype)


def wrap_depth(field):
    return jnp.concatenate([field[:, :, :, -1:], field, field[:, :, :, :1]], axis=3)


def forward_import(field):
    column = passed_along(field[:, :1], "gx", -1)
    widened = jnp.concatenate([field, column], axis=1)
    rows = with_halo(widened, (("gy", 2),), 1)
    return wrap_depth(rows)


def return_sums(buffer):
    core = buffer[:, :, :, 1:-1]
    core = core.at[:, :, :, -1].add(buffer[:, :, :, 0])
    core = core.at[:, :, :, 0].add(buffer[:, :, :, -1])
    lower = passed_along(core[:, :, 0], "gy", -1)
    upper = passed_along(core[:, :, -1], "gy", 1)
    core = core.at[:, :, -2].add(lower)
    core = core.at[:, :, 1].add(upper)
    inner = core[:, :, 1:-1]
    back = passed_along(inner[:, -1], "gx", 1)
    inner = inner.at[:, 0].add(back)
    return inner[:, :-1]


def forward_offsets():
    listed = []
    for step_x in (0, 1):
        for step_y in (-1, 0, 1):
            for step_z in (-1, 0, 1):
                if (step_x, step_y, step_z) > (0, 0, 0):
                    listed.append((step_x, step_y, step_z))
    return listed


def near_block(buffer, offset, widths):
    first, second, third = (offset[0], 1 + offset[1], 1 + offset[2])
    return buffer[
        :, first : first + widths[0], second : second + widths[1], third : third + widths[2], :
    ]


def add_block(buffer, offset, value):
    first, second, third = (offset[0], 1 + offset[1], 1 + offset[2])
    shape = value.shape
    return buffer.at[
        :, first : first + shape[1], second : second + shape[2], third : third + shape[3], :
    ].add(value)


def pair_geometry(positions, filled_own, outer, offset, selfish):
    widths = positions.shape[1:4]
    near = near_block(outer, offset, widths)
    parts = []
    for component in range(3):
        moved = near[component] + float(offset[component])
        parts.append(moved[..., None, :] - positions[component][..., :, None])
    square = parts[0] * parts[0] + parts[1] * parts[1] + parts[2] * parts[2]
    reach = jnp.maximum(1.0 - square, 0.0)
    weights_mask = filled_own[..., :, None] * near[3][..., None, :]
    if selfish:
        slots = positions.shape[-1]
        weights_mask = weights_mask * (1.0 - jnp.eye(slots, dtype=positions.dtype))
    return (parts, reach, weights_mask)


def forces_once(positions, amount):
    slots = positions.shape[-1]
    widths = positions.shape[1:4]
    filled_own = slots_filled(amount, slots)
    packed = jnp.concatenate([positions, filled_own[None]], axis=0)
    outer = forward_import(packed)
    shape_ext = (widths[0] + 1, widths[1] + 2, widths[2] + 2, slots)
    offsets = forward_offsets()
    anchor = (0, 0, 0)
    gathered = jnp.zeros((1,) + shape_ext, jnp.float32)
    parts, reach, weights_mask = pair_geometry(positions, filled_own, outer, anchor, True)
    gathered = add_block(gathered, anchor, jnp.sum(weights_mask * reach * reach, axis=-1)[None])
    for offset in offsets:
        parts, reach, weights_mask = pair_geometry(positions, filled_own, outer, offset, False)
        term = weights_mask * reach * reach
        gathered = add_block(gathered, anchor, jnp.sum(term, axis=-1)[None])
        gathered = add_block(gathered, offset, jnp.sum(term, axis=-2)[None])
    density = DENSITY_SCALE * return_sums(gathered)[0]
    slope = -0.5 / jnp.sqrt(1.0 + density)
    slope_outer = forward_import(slope[None])

    def coupled(offset, selfish):
        parts, reach, weights_mask = pair_geometry(positions, filled_own, outer, offset, selfish)
        slope_near = near_block(slope_outer, offset, widths)[0]
        both = slope[..., :, None] + slope_near[..., None, :]
        coupling = (
            2.0
            * weights_mask
            * reach
            * (-2.0 * DENSITY_SCALE * both - 4.0 * PAIR_SCALE * reach * reach)
        )
        return (parts, coupling)

    pushed = jnp.zeros((3,) + shape_ext, jnp.float32)
    parts, coupling = coupled(anchor, True)
    own_side = jnp.stack([jnp.sum(coupling * parts[component], axis=-1) for component in range(3)])
    pushed = add_block(pushed, anchor, own_side)
    for offset in offsets:
        parts, coupling = coupled(offset, False)
        own_side = jnp.stack(
            [jnp.sum(coupling * parts[component], axis=-1) for component in range(3)]
        )
        other_side = jnp.stack(
            [jnp.sum(coupling * parts[component], axis=-2) for component in range(3)]
        )
        pushed = add_block(pushed, anchor, own_side)
        pushed = add_block(pushed, offset, -other_side)
    return return_sums(pushed) * filled_own[None]


def forces_of(positions, amount):
    return forces_once(positions, amount)


def shards(positions, velocities, counts):
    amount = counts.astype(jnp.float32)
    pushed = forces_of(positions, amount)

    def verlet_step(step_index, state):
        places, speeds, pulled = state
        speeds = speeds + 0.5 * TIME_STEP * pulled
        places = places + TIME_STEP * speeds
        pulled = forces_of(places, amount)
        speeds = speeds + 0.5 * TIME_STEP * pulled
        return (places, speeds, pulled)

    positions, velocities, pushed = lax.fori_loop(
        0, STEPS, verlet_step, (positions, velocities, pushed)
    )
    return (positions, velocities, pushed)


def solution(mesh):
    in_specs = (
        P(None, "gx", "gy", None, None),
        P(None, "gx", "gy", None, None),
        P("gx", "gy", None),
    )
    out_specs = (
        P(None, "gx", "gy", None, None),
        P(None, "gx", "gy", None, None),
        P(None, "gx", "gy", None, None),
    )
    return jax.shard_map(shards, mesh=mesh, in_specs=in_specs, out_specs=out_specs, check_vma=False)
```

profile of v0, /device:TPU:0, one launch (start us, length us, event | category | flops | bytes accessed | tf_op | source)
XLA Modules:
  0.0 374.0 jit_solution(10070177395588335727)
XLA Ops:
  2.3 5.5 %collective-permute-start.12 = (f32[4,1,2,12,128]{4,0,3,2,1:T(4,128)S(1)}, f32[4,1,2,12,128]{4,0,3,2,1:T(4,128)S(1)}, u32[]{:S(2)}, u32[]{:S(2)}) collective-permute-start(f32[4,1,2,12,128]{4,0,3,2,1:T(4,128)S(1)} %pad_maximum_fusion.49), channel_id=1, source_target_pairs={{2,0},{4,2},{6,4},{8,6},{10,8},{12,10},{14,12},{16,14},{18,16},{20... | collective-permute-start | bytes 147464 | tf_op jit(solution)/shard_map/ppermute | solution.py:17
  9.5 1.6 collective-permute-start.13
  17.4 5.0 %fusion.460 = (f32[2,12,128]{2,1,0:T(8,128)S(1)}, f32[2,12,128]{2,1,0:T(8,128)S(1)}, f32[2,12,128]{2,1,0:T(8,128)S(1)}, f32[2,12,128]{2,1,0:T(8,128)S(1)}, f32[2...) fusion(f32[2,12,128]{2,1,0:T(8,128)S(1)} %copy.1827, f32[2,12,128]{2,1,0:T(8,128)S(1)} %copy.1825, ...), kind=kLoop, calls=%fused_computation.950 | loop fusion | flops 23571456 | bytes 348160 | tf_op jit(solution)/shard_map/reduce_sum | solution.py:120
  22.6 2.0 bitcast_add_fusion.2
  24.6 2.1 scatter-add.416
  26.9 4.2 %fusion.458 = (f32[2,12,128]{2,1,0:T(8,128)S(1)}, f32[2,12,128]{2,1,0:T(8,128)S(1)}, f32[2,12,128]{2,1,0:T(8,128)S(1)}, f32[2,12,128]{2,1,0:T(8,128)S(1)}, f32[2...) fusion(f32[2,12,128]{2,1,0:T(8,128)S(1)} %copy.1817, f32[2,12,128]{2,1,0:T(8,128)S(1)} %copy.1815, ...), kind=kLoop, calls=%fused_computation.948 | loop fusion | flops 17676288 | bytes 270336 | tf_op jit(solution)/shard_map/reduce_sum | solution.py:120
  31.5 4.2 %fusion.456 = (f32[2,12,128]{2,1,0:T(8,128)S(1)}, f32[2,12,128]{2,1,0:T(8,128)S(1)}, f32[2,12,128]{2,1,0:T(8,128)S(1)}, f32[2,12,128]{2,1,0:T(8,128)S(1)}, f32[2...) fusion(f32[2,12,128]{2,1,0:T(8,128)S(1)} %copy.1807, f32[2,12,128]{2,1,0:T(8,128)S(1)} %copy.1805, ...), kind=kLoop, calls=%fused_computation.946 | loop fusion | flops 17676288 | bytes 270336 | tf_op jit(solution)/shard_map/reduce_sum | solution.py:120
  36.1 4.2 %fusion.454 = (f32[2,12,128]{2,1,0:T(8,128)S(1)}, f32[2,12,128]{2,1,0:T(8,128)S(1)}, f32[2,12,128]{2,1,0:T(8,128)S(1)}, f32[2,12,128]{2,1,0:T(8,128)S(1)}, f32[2...) fusion(f32[2,12,128]{2,1,0:T(8,128)S(1)} %copy.1797, f32[2,12,128]{2,1,0:T(8,128)S(1)} %copy.1795, ...), kind=kLoop, calls=%fused_computation.944 | loop fusion | flops 17676288 | bytes 270336 | tf_op jit(solution)/shard_map/reduce_sum | solution.py:120
  40.9 2.5 fusion.452
  49.5 5.8 %collective-permute-done.17 = f32[1,2,12,128]{3,0,2,1:T(1,128)S(1)} collective-permute-done((f32[1,2,12,128]{3,0,2,1:T(1,128)S(1)}, f32[1,2,12,128]{3,0,2,1:T(1,128)S(1)}, u32[]{:S(2)}, u32[]{:S(2)}) %collective-permute-start.17) | collective-permute-done | bytes 12320 | tf_op jit(solution)/shard_map/ppermute | solution.py:17
  62.5 6.0 %fusion.424 = (f32[2,12,128]{2,1,0:T(8,128)S(1)}, f32[2,12,128]{2,1,0:T(8,128)S(1)}, f32[2,12,128]{2,1,0:T(8,128)S(1)}, f32[2,12,128]{2,1,0:T(8,128)S(1)}, f32[2...) fusion(f32[2,12,128]{2,1,0:T(8,128)S(1)} %copy.1813, ...), kind=kLoop, calls=%fused_computation.914 | loop fusion | flops 21983232 | bytes 331776 | tf_op jit(solution)/shard_map/reduce_sum | solution.py:147
  68.8 6.0 %fusion.406 = (f32[2,12,128]{2,1,0:T(8,128)S(1)}, f32[2,12,128]{2,1,0:T(8,128)S(1)}, f32[2,12,128]{2,1,0:T(8,128)S(1)}, f32[2,12,128]{2,1,0:T(8,128)S(1)}, f32[2...) fusion(f32[2,12,128]{2,1,0:T(8,128)S(1)} %copy.1783, ...), kind=kLoop, calls=%fused_computation.896 | loop fusion | flops 21983232 | bytes 331776 | tf_op jit(solution)/shard_map/reduce_sum | solution.py:147
  75.3 4.1 %fusion.394 = (f32[2,12,128]{2,1,0:T(8,128)S(1)}, f32[2,12,128]{2,1,0:T(8,128)S(1)}, f32[2,12,128]{2,1,0:T(8,128)S(1)}, f32[2,12,128]{2,1,0:T(8,128)S(1)}, f32[2...) fusion(f32[2,12,128]{2,1,0:T(8,128)S(1)} %copy.1763, f32[2,12,128]{2,1,0:T(8,128)S(1)} %copy.1692, ...), kind=kLoop, calls=%fused_computation.884 | loop fusion | flops 10991616 | bytes 196608 | tf_op jit(solution)/shard_map/reduce_sum | solution.py:147
  79.5 8.9 %fusion.430 = (f32[2,12,128]{2,1,0:T(8,128)S(1)}, f32[2,12,128]{2,1,0:T(8,128)S(1)}, f32[2,12,128]{2,1,0:T(8,128)S(1)}, f32[2,12,128]{2,1,0:T(8,128)S(1)}, f32[2...) fusion(f32[2,12,128]{2,1,0:T(8,128)S(1)} %copy.1823, ...), kind=kLoop, calls=%fused_computation.920 | loop fusion | flops 32197632 | bytes 434176 | tf_op jit(solution)/shard_map/reduce_sum | solution.py:147
  88.7 6.0 %fusion.400 = (f32[2,12,128]{2,1,0:T(8,128)S(1)}, f32[2,12,128]{2,1,0:T(8,128)S(1)}, f32[2,12,128]{2,1,0:T(8,128)S(1)}, f32[2,12,128]{2,1,0:T(8,128)S(1)}, f32[2...) fusion(f32[2,12,128]{2,1,0:T(8,128)S(1)} %copy.1773, ...), kind=kLoop, calls=%fused_computation.890 | loop fusion | flops 21983232 | bytes 331776 | tf_op jit(solution)/shard_map/reduce_sum | solution.py:147
  94.9 6.0 %fusion.412 = (f32[2,12,128]{2,1,0:T(8,128)S(1)}, f32[2,12,128]{2,1,0:T(8,128)S(1)}, f32[2,12,128]{2,1,0:T(8,128)S(1)}, f32[2,12,128]{2,1,0:T(8,128)S(1)}, f32[2...) fusion(f32[2,12,128]{2,1,0:T(8,128)S(1)} %copy.1793, ...), kind=kLoop, calls=%fused_computation.902 | loop fusion | flops 21983232 | bytes 331776 | tf_op jit(solution)/shard_map/reduce_sum | solution.py:147
  101.0 6.0 %fusion.418 = (f32[2,12,128]{2,1,0:T(8,128)S(1)}, f32[2,12,128]{2,1,0:T(8,128)S(1)}, f32[2,12,128]{2,1,0:T(8,128)S(1)}, f32[2,12,128]{2,1,0:T(8,128)S(1)}, f32[2...) fusion(f32[2,12,128]{2,1,0:T(8,128)S(1)} %copy.1803, ...), kind=kLoop, calls=%fused_computation.908 | loop fusion | flops 21983232 | bytes 331776 | tf_op jit(solution)/shard_map/reduce_sum | solution.py:147
  107.8 2.0 fusion.474
  109.7 2.2 scatter-add.469
  119.6 1.8 collective-permute-done.21
  122.4 6.0 %collective-permute-done.23 = f32[3,2,12,128]{3,1,2,0:T(2,128)S(1)} collective-permute-done((f32[3,2,12,128]{3,1,2,0:T(2,128)S(1)}, f32[3,2,12,128]{3,1,2,0:T(2,128)S(1)}, u32[]{:S(2)}, u32[]{:S(2)}) %collective-permute-start.23) | collective-permute-done | bytes 36896 | tf_op jit(solution)/shard_map/ppermute | solution.py:17
  128.5 243.4 %while.145 = (s32[]{:T(128)}, f32[3,1,2,12,128]{4,0,3,2,1:T(4,128)S(1)}, f32[3,1,2,12,128]{4,0,3,2,1:T(4,128)S(1)}, f32[3,1,2,12,128]{4,0,3,2,1:T(4,128)S(1)}, f...) while((s32[]{:T(128)}, f32[3,1,2,12,128]{4,0,3,2,1:T(4,128)S(1)}, ...), condition=%wide.region_217.218_spmd, body=%wide.region_108.217_spmd.sunk | while | flops 238132224 | bytes 23204740 | solution.py:170
  141.7 1.7 collective-permute-done
  146.2 1.8 collective-permute-done.1
  151.3 5.0 %fusion.574 = (f32[2,12,128]{2,1,0:T(8,128)S(1)}, f32[2,12,128]{2,1,0:T(8,128)S(1)}, f32[2,12,128]{2,1,0:T(8,128)S(1)}, f32[2,12,128]{2,1,0:T(8,128)S(1)}, f32[2...) fusion(f32[2,12,128]{2,1,0:T(8,128)S(1)} %copy.2814, ...), kind=kLoop, calls=%fused_computation.329.clone.1 | loop fusion | flops 23571456 | bytes 348160 | tf_op jit(solution)/shard_map/while/body/eval_jaxpr/reduce_sum | solution.py:120
  156.6 2.0 bitcast_add_fusion.7
  158.6 2.1 scatter-add.868
  161.0 4.2 %fusion.577 = (f32[2,12,128]{2,1,0:T(8,128)S(1)}, f32[2,12,128]{2,1,0:T(8,128)S(1)}, f32[2,12,128]{2,1,0:T(8,128)S(1)}, f32[2,12,128]{2,1,0:T(8,128)S(1)}, f32[2...) fusion(f32[2,12,128]{2,1,0:T(8,128)S(1)} %copy.2833, f32[2,12,128]{2,1,0:T(8,128)S(1)} %copy.2834, ...), kind=kLoop, calls=%fused_computation.327.clone.1 | loop fusion | flops 17676288 | bytes 270336 | tf_op jit(solution)/shard_map/while/body/eval_jaxpr/reduce_sum | solution.py:120
  165.6 4.2 %fusion.581 = (f32[2,12,128]{2,1,0:T(8,128)S(1)}, f32[2,12,128]{2,1,0:T(8,128)S(1)}, f32[2,12,128]{2,1,0:T(8,128)S(1)}, f32[2,12,128]{2,1,0:T(8,128)S(1)}, f32[2...) fusion(f32[2,12,128]{2,1,0:T(8,128)S(1)} %copy.2848, f32[2,12,128]{2,1,0:T(8,128)S(1)} %copy.2850, ...), kind=kLoop, calls=%fused_computation.325.clone.1 | loop fusion | flops 17676288 | bytes 270336 | tf_op jit(solution)/shard_map/while/body/eval_jaxpr/reduce_sum | solution.py:120
  170.2 4.2 %fusion.584 = (f32[2,12,128]{2,1,0:T(8,128)S(1)}, f32[2,12,128]{2,1,0:T(8,128)S(1)}, f32[2,12,128]{2,1,0:T(8,128)S(1)}, f32[2,12,128]{2,1,0:T(8,128)S(1)}, f32[2...) fusion(f32[2,12,128]{2,1,0:T(8,128)S(1)} %copy.2868, f32[2,12,128]{2,1,0:T(8,128)S(1)} %copy.2869, ...), kind=kLoop, calls=%fused_computation.323.clone.1 | loop fusion | flops 17676288 | bytes 270336 | tf_op jit(solution)/shard_map/while/body/eval_jaxpr/reduce_sum | solution.py:120
  175.0 2.5 fusion.586
  181.2 1.6 collective-permute-done.3
  183.5 5.8 %collective-permute-done.5 = f32[1,2,12,128]{3,0,2,1:T(1,128)S(1)} collective-permute-done((f32[1,2,12,128]{3,0,2,1:T(1,128)S(1)}, f32[1,2,12,128]{3,0,2,1:T(1,128)S(1)}, u32[]{:S(2)}, u32[]{:S(2)}) %collective-permute-start.5) | collective-permute-done | bytes 12320 | tf_op jit(solution)/shard_map/while/body/eval_jaxpr/ppermute | solution.py:17
  196.3 6.0 %fusion.610 = (f32[2,12,128]{2,1,0:T(8,128)S(1)}, f32[2,12,128]{2,1,0:T(8,128)S(1)}, f32[2,12,128]{2,1,0:T(8,128)S(1)}, f32[2,12,128]{2,1,0:T(8,128)S(1)}, f32[2...) fusion(f32[2,12,128]{2,1,0:T(8,128)S(1)} %copy.2878, ...), kind=kLoop, calls=%fused_computation.269.clone.1 | loop fusion | flops 21983232 | bytes 331776 | tf_op jit(solution)/shard_map/while/body/eval_jaxpr/reduce_sum | solution.py:147
  203.0 4.1 %fusion.613 = (f32[2,12,128]{2,1,0:T(8,128)S(1)}, f32[2,12,128]{2,1,0:T(8,128)S(1)}, f32[2,12,128]{2,1,0:T(8,128)S(1)}, f32[2,12,128]{2,1,0:T(8,128)S(1)}, f32[2...) fusion(f32[2,12,128]{2,1,0:T(8,128)S(1)} %copy.2874, f32[2,12,128]{2,1,0:T(8,128)S(1)} %copy.2813, ...), kind=kLoop, calls=%fused_computation.263.clone.1 | loop fusion | flops 10991616 | bytes 196608 | tf_op jit(solution)/shard_map/while/body/eval_jaxpr/reduce_sum | solution.py:147
  207.2 8.9 %fusion.595 = (f32[2,12,128]{2,1,0:T(8,128)S(1)}, f32[2,12,128]{2,1,0:T(8,128)S(1)}, f32[2,12,128]{2,1,0:T(8,128)S(1)}, f32[2,12,128]{2,1,0:T(8,128)S(1)}, f32[2...) fusion(f32[2,12,128]{2,1,0:T(8,128)S(1)} %copy.2812, ...), kind=kLoop, calls=%fused_computation.299.clone.1 | loop fusion | flops 32197632 | bytes 434176 | tf_op jit(solution)/shard_map/while/body/eval_jaxpr/reduce_sum | solution.py:147
  216.5 6.0 %fusion.607 = (f32[2,12,128]{2,1,0:T(8,128)S(1)}, f32[2,12,128]{2,1,0:T(8,128)S(1)}, f32[2,12,128]{2,1,0:T(8,128)S(1)}, f32[2,12,128]{2,1,0:T(8,128)S(1)}, f32[2...) fusion(f32[2,12,128]{2,1,0:T(8,128)S(1)} %copy.2882, ...), kind=kLoop, calls=%fused_computation.275.clone.1 | loop fusion | flops 21983232 | bytes 331776 | tf_op jit(solution)/shard_map/while/body/eval_jaxpr/reduce_sum | solution.py:147
  222.7 6.0 %fusion.601 = (f32[2,12,128]{2,1,0:T(8,128)S(1)}, f32[2,12,128]{2,1,0:T(8,128)S(1)}, f32[2,12,128]{2,1,0:T(8,128)S(1)}, f32[2,12,128]{2,1,0:T(8,128)S(1)}, f32[2...) fusion(f32[2,12,128]{2,1,0:T(8,128)S(1)} %copy.2852, ...), kind=kLoop, calls=%fused_computation.287.clone.1 | loop fusion | flops 21983232 | bytes 331776 | tf_op jit(solution)/shard_map/while/body/eval_jaxpr/reduce_sum | solution.py:147
  229.0 6.0 %fusion.598 = (f32[2,12,128]{2,1,0:T(8,128)S(1)}, f32[2,12,128]{2,1,0:T(8,128)S(1)}, f32[2,12,128]{2,1,0:T(8,128)S(1)}, f32[2,12,128]{2,1,0:T(8,128)S(1)}, f32[2...) fusion(f32[2,12,128]{2,1,0:T(8,128)S(1)} %copy.2835, ...), kind=kLoop, calls=%fused_computation.293.clone.1 | loop fusion | flops 21983232 | bytes 331776 | tf_op jit(solution)/shard_map/while/body/eval_jaxpr/reduce_sum | solution.py:147
  235.1 6.0 %fusion.604 = (f32[2,12,128]{2,1,0:T(8,128)S(1)}, f32[2,12,128]{2,1,0:T(8,128)S(1)}, f32[2,12,128]{2,1,0:T(8,128)S(1)}, f32[2,12,128]{2,1,0:T(8,128)S(1)}, f32[2...) fusion(f32[2,12,128]{2,1,0:T(8,128)S(1)} %copy.2870, ...), kind=kLoop, calls=%fused_computation.281.clone.1 | loop fusion | flops 21983232 | bytes 331776 | tf_op jit(solution)/shard_map/while/body/eval_jaxpr/reduce_sum | solution.py:147
  241.8 2.0 fusion.597
  247.7 2.0 collective-permute-done.9
  250.4 6.2 %collective-permute-done.11 = f32[3,2,12,128]{3,0,2,1:T(4,128)S(1)} collective-permute-done((f32[3,2,12,128]{3,0,2,1:T(4,128)S(1)}, f32[3,2,12,128]{3,0,2,1:T(4,128)S(1)}, u32[]{:S(2)}, u32[]{:S(2)}) %collective-permute-start.11) | collective-permute-done | bytes 36896 | tf_op jit(solution)/shard_map/while/body/eval_jaxpr/ppermute | solution.py:17
  257.0 1.7 collective-permute-done
  261.5 1.8 collective-permute-done.1
  266.6 5.0 %fusion.574 = (f32[2,12,128]{2,1,0:T(8,128)S(1)}, f32[2,12,128]{2,1,0:T(8,128)S(1)}, f32[2,12,128]{2,1,0:T(8,128)S(1)}, f32[2,12,128]{2,1,0:T(8,128)S(1)}, f32[2...) fusion(f32[2,12,128]{2,1,0:T(8,128)S(1)} %copy.2814, ...), kind=kLoop, calls=%fused_computation.329.clone.1 | loop fusion | flops 23571456 | bytes 348160 | tf_op jit(solution)/shard_map/while/body/eval_jaxpr/reduce_sum | solution.py:120
  271.9 2.0 bitcast_add_fusion.7
  273.9 2.1 scatter-add.868
  276.2 4.2 %fusion.577 = (f32[2,12,128]{2,1,0:T(8,128)S(1)}, f32[2,12,128]{2,1,0:T(8,128)S(1)}, f32[2,12,128]{2,1,0:T(8,128)S(1)}, f32[2,12,128]{2,1,0:T(8,128)S(1)}, f32[2...) fusion(f32[2,12,128]{2,1,0:T(8,128)S(1)} %copy.2833, f32[2,12,128]{2,1,0:T(8,128)S(1)} %copy.2834, ...), kind=kLoop, calls=%fused_computation.327.clone.1 | loop fusion | flops 17676288 | bytes 270336 | tf_op jit(solution)/shard_map/while/body/eval_jaxpr/reduce_sum | solution.py:120
  280.9 4.2 %fusion.581 = (f32[2,12,128]{2,1,0:T(8,128)S(1)}, f32[2,12,128]{2,1,0:T(8,128)S(1)}, f32[2,12,128]{2,1,0:T(8,128)S(1)}, f32[2,12,128]{2,1,0:T(8,128)S(1)}, f32[2...) fusion(f32[2,12,128]{2,1,0:T(8,128)S(1)} %copy.2848, f32[2,12,128]{2,1,0:T(8,128)S(1)} %copy.2850, ...), kind=kLoop, calls=%fused_computation.325.clone.1 | loop fusion | flops 17676288 | bytes 270336 | tf_op jit(solution)/shard_map/while/body/eval_jaxpr/reduce_sum | solution.py:120
  285.5 4.2 %fusion.584 = (f32[2,12,128]{2,1,0:T(8,128)S(1)}, f32[2,12,128]{2,1,0:T(8,128)S(1)}, f32[2,12,128]{2,1,0:T(8,128)S(1)}, f32[2,12,128]{2,1,0:T(8,128)S(1)}, f32[2...) fusion(f32[2,12,128]{2,1,0:T(8,128)S(1)} %copy.2868, f32[2,12,128]{2,1,0:T(8,128)S(1)} %copy.2869, ...), kind=kLoop, calls=%fused_computation.323.clone.1 | loop fusion | flops 17676288 | bytes 270336 | tf_op jit(solution)/shard_map/while/body/eval_jaxpr/reduce_sum | solution.py:120
  290.3 2.5 fusion.586
  296.5 1.6 collective-permute-done.3
  298.8 5.8 %collective-permute-done.5 = f32[1,2,12,128]{3,0,2,1:T(1,128)S(1)} collective-permute-done((f32[1,2,12,128]{3,0,2,1:T(1,128)S(1)}, f32[1,2,12,128]{3,0,2,1:T(1,128)S(1)}, u32[]{:S(2)}, u32[]{:S(2)}) %collective-permute-start.5) | collective-permute-done | bytes 12320 | tf_op jit(solution)/shard_map/while/body/eval_jaxpr/ppermute | solution.py:17
  311.6 6.0 %fusion.610 = (f32[2,12,128]{2,1,0:T(8,128)S(1)}, f32[2,12,128]{2,1,0:T(8,128)S(1)}, f32[2,12,128]{2,1,0:T(8,128)S(1)}, f32[2,12,128]{2,1,0:T(8,128)S(1)}, f32[2...) fusion(f32[2,12,128]{2,1,0:T(8,128)S(1)} %copy.2878, ...), kind=kLoop, calls=%fused_computation.269.clone.1 | loop fusion | flops 21983232 | bytes 331776 | tf_op jit(solution)/shard_map/while/body/eval_jaxpr/reduce_sum | solution.py:147
  318.2 4.1 %fusion.613 = (f32[2,12,128]{2,1,0:T(8,128)S(1)}, f32[2,12,128]{2,1,0:T(8,128)S(1)}, f32[2,12,128]{2,1,0:T(8,128)S(1)}, f32[2,12,128]{2,1,0:T(8,128)S(1)}, f32[2...) fusion(f32[2,12,128]{2,1,0:T(8,128)S(1)} %copy.2874, f32[2,12,128]{2,1,0:T(8,128)S(1)} %copy.2813, ...), kind=kLoop, calls=%fused_computation.263.clone.1 | loop fusion | flops 10991616 | bytes 196608 | tf_op jit(solution)/shard_map/while/body/eval_jaxpr/reduce_sum | solution.py:147
  322.5 8.9 %fusion.595 = (f32[2,12,128]{2,1,0:T(8,128)S(1)}, f32[2,12,128]{2,1,0:T(8,128)S(1)}, f32[2,12,128]{2,1,0:T(8,128)S(1)}, f32[2,12,128]{2,1,0:T(8,128)S(1)}, f32[2...) fusion(f32[2,12,128]{2,1,0:T(8,128)S(1)} %copy.2812, ...), kind=kLoop, calls=%fused_computation.299.clone.1 | loop fusion | flops 32197632 | bytes 434176 | tf_op jit(solution)/shard_map/while/body/eval_jaxpr/reduce_sum | solution.py:147
  331.7 6.0 %fusion.607 = (f32[2,12,128]{2,1,0:T(8,128)S(1)}, f32[2,12,128]{2,1,0:T(8,128)S(1)}, f32[2,12,128]{2,1,0:T(8,128)S(1)}, f32[2,12,128]{2,1,0:T(8,128)S(1)}, f32[2...) fusion(f32[2,12,128]{2,1,0:T(8,128)S(1)} %copy.2882, ...), kind=kLoop, calls=%fused_computation.275.clone.1 | loop fusion | flops 21983232 | bytes 331776 | tf_op jit(solution)/shard_map/while/body/eval_jaxpr/reduce_sum | solution.py:147
  338.0 6.0 %fusion.601 = (f32[2,12,128]{2,1,0:T(8,128)S(1)}, f32[2,12,128]{2,1,0:T(8,128)S(1)}, f32[2,12,128]{2,1,0:T(8,128)S(1)}, f32[2,12,128]{2,1,0:T(8,128)S(1)}, f32[2...) fusion(f32[2,12,128]{2,1,0:T(8,128)S(1)} %copy.2852, ...), kind=kLoop, calls=%fused_computation.287.clone.1 | loop fusion | flops 21983232 | bytes 331776 | tf_op jit(solution)/shard_map/while/body/eval_jaxpr/reduce_sum | solution.py:147
  344.3 6.0 %fusion.598 = (f32[2,12,128]{2,1,0:T(8,128)S(1)}, f32[2,12,128]{2,1,0:T(8,128)S(1)}, f32[2,12,128]{2,1,0:T(8,128)S(1)}, f32[2,12,128]{2,1,0:T(8,128)S(1)}, f32[2...) fusion(f32[2,12,128]{2,1,0:T(8,128)S(1)} %copy.2835, ...), kind=kLoop, calls=%fused_computation.293.clone.1 | loop fusion | flops 21983232 | bytes 331776 | tf_op jit(solution)/shard_map/while/body/eval_jaxpr/reduce_sum | solution.py:147
  350.4 6.0 %fusion.604 = (f32[2,12,128]{2,1,0:T(8,128)S(1)}, f32[2,12,128]{2,1,0:T(8,128)S(1)}, f32[2,12,128]{2,1,0:T(8,128)S(1)}, f32[2,12,128]{2,1,0:T(8,128)S(1)}, f32[2...) fusion(f32[2,12,128]{2,1,0:T(8,128)S(1)} %copy.2870, ...), kind=kLoop, calls=%fused_computation.281.clone.1 | loop fusion | flops 21983232 | bytes 331776 | tf_op jit(solution)/shard_map/while/body/eval_jaxpr/reduce_sum | solution.py:147
  357.1 2.0 fusion.597
  363.0 2.0 collective-permute-done.9
  365.7 6.2 %collective-permute-done.11 = f32[3,2,12,128]{3,0,2,1:T(4,128)S(1)} collective-permute-done((f32[3,2,12,128]{3,0,2,1:T(4,128)S(1)}, f32[3,2,12,128]{3,0,2,1:T(4,128)S(1)}, u32[]{:S(2)}, u32[]{:S(2)}) %collective-permute-start.11) | collective-permute-done | bytes 36896 | tf_op jit(solution)/shard_map/while/body/eval_jaxpr/ppermute | solution.py:17
  (1051 shorter events, 84.1 us)
Async XLA Ops:
  0.6 7.2 %copy-start = (f32[3,1,2,12,128]{4,2,3,1,0:T(2,128)S(1)}, f32[3,1,2,12,128]{4,2,3,1,0:T(2,128)}, u32[]{:S(2)}) copy-start(f32[3,1,2,12,128]{4,2,3,1,0:T(2,128)} %param.261) | copy-start | bytes 110596
  2.3 7.2 %collective-permute-start.12 = (f32[4,1,2,12,128]{4,0,3,2,1:T(4,128)S(1)}, f32[4,1,2,12,128]{4,0,3,2,1:T(4,128)S(1)}, u32[]{:S(2)}, u32[]{:S(2)}) collective-permute-start(f32[4,1,2,12,128]{4,0,3,2,1:T(4,128)S(1)} %pad_maximum_fusion.49), channel_id=1, source_target_pairs={{2,0},{4,2},{6,4},{8,6},{10,8},{12,10},{14,12},{16,14},{18,16},{20... | collective-permute-start | bytes 147464 | tf_op jit(solution)/shard_map/ppermute | solution.py:17
  9.5 4.2 %collective-permute-start.13 = (f32[4,2,1,12,128]{4,0,3,2,1:T(4,128)S(1)}, f32[4,2,1,12,128]{4,0,3,2,1:T(4,128)S(1)}, u32[]{:S(2)}, u32[]{:S(2)}) collective-permute-start(f32[4,2,1,12,128]{4,0,3,2,1:T(4,128)S(1)} %get-tuple-element.2217), channel_id=1, source_target_pairs={{0,1},{1,0},{2,3},{3,2},{4,5},{5,4},{6,7},{7,6},{8,9},{9,8},{10,11... | collective-permute-start | bytes 147464 | tf_op jit(solution)/shard_map/ppermute | solution.py:27
  11.1 4.1 %collective-permute-start.14 = (f32[4,2,1,12,128]{4,0,3,2,1:T(4,128)S(1)}, f32[4,2,1,12,128]{4,0,3,2,1:T(4,128)S(1)}, u32[]{:S(2)}, u32[]{:S(2)}) collective-permute-start(f32[4,2,1,12,128]{4,0,3,2,1:T(4,128)S(1)} %get-tuple-element.2218), channel_id=1, source_target_pairs={{1,0},{0,1},{3,2},{2,3},{5,4},{4,5},{7,6},{6,7},{9,8},{8,9},{11,10... | collective-permute-start | bytes 147464 | tf_op jit(solution)/shard_map/ppermute | solution.py:28
  45.0 3.8 %collective-permute-start.15 = (f32[1,2,12,128]{3,0,2,1:T(1,128)S(1)}, f32[1,2,12,128]{3,0,2,1:T(1,128)S(1)}, u32[]{:S(2)}, u32[]{:S(2)}) collective-permute-start(f32[1,2,12,128]{3,0,2,1:T(1,128)S(1)} %slice_bitcast_fusion.10), channel_id=1, source_target_pairs={{1,0},{0,1},{3,2},{2,3},{5,4},{4,5},{7,6},{6,7},{9,8},{8,9},{11,10... | collective-permute-start | bytes 36872 | tf_op jit(solution)/shard_map/ppermute | solution.py:17
  45.6 3.8 %collective-permute-start.16 = (f32[1,2,12,128]{3,0,2,1:T(1,128)S(1)}, f32[1,2,12,128]{3,0,2,1:T(1,128)S(1)}, u32[]{:S(2)}, u32[]{:S(2)}) collective-permute-start(f32[1,2,12,128]{3,0,2,1:T(1,128)S(1)} %slice_bitcast_fusion.9), channel_id=1, source_target_pairs={{1,0},{0,1},{3,2},{2,3},{5,4},{4,5},{7,6},{6,7},{9,8},{8,9},{11,10... | collective-permute-start | bytes 36872 | tf_op jit(solution)/shard_map/ppermute | solution.py:17
  49.4 5.9 %collective-permute-start.17 = (f32[1,2,12,128]{3,0,2,1:T(1,128)S(1)}, f32[1,2,12,128]{3,0,2,1:T(1,128)S(1)}, u32[]{:S(2)}, u32[]{:S(2)}) collective-permute-start(f32[1,2,12,128]{3,0,2,1:T(1,128)S(1)} %slice_bitcast_fusion.8), channel_id=1, source_target_pairs={{30,0},{0,2},{2,4},{4,6},{6,8},{8,10},{10,12},{12,14},{14,16},{16,... | collective-permute-start | bytes 36872 | tf_op jit(solution)/shard_map/ppermute | solution.py:17
  55.3 1.7 collective-permute-start.18
  57.1 3.8 %collective-permute-start.20 = (f32[1,2,1,12,128]{4,0,3,2,1:T(1,128)S(1)}, f32[1,2,1,12,128]{4,0,3,2,1:T(1,128)S(1)}, u32[]{:S(2)}, u32[]{:S(2)}) collective-permute-start(f32[1,2,1,12,128]{4,0,3,2,1:T(1,128)S(1)} %get-tuple-element.2241), channel_id=1, source_target_pairs={{1,0},{0,1},{3,2},{2,3},{5,4},{4,5},{7,6},{6,7},{9,8},{8,9},{11,10... | collective-permute-start | bytes 36872 | tf_op jit(solution)/shard_map/ppermute | solution.py:28
  58.7 3.8 %collective-permute-start.19 = (f32[1,2,1,12,128]{4,0,3,2,1:T(1,128)S(1)}, f32[1,2,1,12,128]{4,0,3,2,1:T(1,128)S(1)}, u32[]{:S(2)}, u32[]{:S(2)}) collective-permute-start(f32[1,2,1,12,128]{4,0,3,2,1:T(1,128)S(1)} %get-tuple-element.2240), channel_id=1, source_target_pairs={{0,1},{1,0},{2,3},{3,2},{4,5},{5,4},{6,7},{7,6},{8,9},{9,8},{10,11... | collective-permute-start | bytes 36872 | tf_op jit(solution)/shard_map/ppermute | solution.py:27
  117.4 4.0 %collective-permute-start.21 = (f32[3,2,12,128]{3,1,2,0:T(2,128)S(1)}, f32[3,2,12,128]{3,1,2,0:T(2,128)S(1)}, u32[]{:S(2)}, u32[]{:S(2)}) collective-permute-start(f32[3,2,12,128]{3,1,2,0:T(2,128)S(1)} %bitcast.1417), channel_id=1, source_target_pairs={{1,0},{0,1},{3,2},{2,3},{5,4},{4,5},{7,6},{6,7},{9,8},{8,9},{11,10... | collective-permute-start | bytes 110600 | tf_op jit(solution)/shard_map/ppermute | solution.py:17
  118.0 4.4 %copy-start.1 = (f32[3,1,2,12,128]{4,2,3,1,0:T(2,128)S(1)}, f32[3,1,2,12,128]{4,2,3,1,0:T(2,128)}, u32[]{:S(2)}) copy-start(f32[3,1,2,12,128]{4,2,3,1,0:T(2,128)} %param.262) | copy-start | bytes 110596
  118.0 4.0 %collective-permute-start.22 = (f32[3,2,12,128]{3,1,2,0:T(2,128)S(1)}, f32[3,2,12,128]{3,1,2,0:T(2,128)S(1)}, u32[]{:S(2)}, u32[]{:S(2)}) collective-permute-start(f32[3,2,12,128]{3,1,2,0:T(2,128)S(1)} %bitcast.1416), channel_id=1, source_target_pairs={{1,0},{0,1},{3,2},{2,3},{5,4},{4,5},{7,6},{6,7},{9,8},{8,9},{11,10... | collective-permute-start | bytes 110600 | tf_op jit(solution)/shard_map/ppermute | solution.py:17
  122.3 6.1 %collective-permute-start.23 = (f32[3,2,12,128]{3,1,2,0:T(2,128)S(1)}, f32[3,2,12,128]{3,1,2,0:T(2,128)S(1)}, u32[]{:S(2)}, u32[]{:S(2)}) collective-permute-start(f32[3,2,12,128]{3,1,2,0:T(2,128)S(1)} %slice_bitcast_fusion.7), channel_id=1, source_target_pairs={{30,0},{0,2},{2,4},{4,6},{6,8},{8,10},{10,12},{12,14},{14,16},{16,... | collective-permute-start | bytes 110600 | tf_op jit(solution)/shard_map/ppermute | solution.py:17
  141.6 1.8 collective-permute-start
  143.4 4.6 %collective-permute-start.1 = (f32[4,2,1,12,128]{4,0,3,2,1:T(4,128)S(1)}, f32[4,2,1,12,128]{4,0,3,2,1:T(4,128)S(1)}, u32[]{:S(2)}, u32[]{:S(2)}) collective-permute-start(f32[4,2,1,12,128]{4,0,3,2,1:T(4,128)S(1)} %get-tuple-element.2527), channel_id=1, source_target_pairs={{1,0},{0,1},{3,2},{2,3},{5,4},{4,5},{7,6},{6,7},{9,8},{8,9},{11,10... | collective-permute-start | bytes 147464 | tf_op jit(solution)/shard_map/while/body/eval_jaxpr/ppermute | solution.py:28
  145.0 4.1 %collective-permute-start.2 = (f32[4,2,1,12,128]{4,0,3,2,1:T(4,128)S(1)}, f32[4,2,1,12,128]{4,0,3,2,1:T(4,128)S(1)}, u32[]{:S(2)}, u32[]{:S(2)}) collective-permute-start(f32[4,2,1,12,128]{4,0,3,2,1:T(4,128)S(1)} %get-tuple-element.2528), channel_id=1, source_target_pairs={{0,1},{1,0},{2,3},{3,2},{4,5},{5,4},{6,7},{7,6},{8,9},{9,8},{10,11... | collective-permute-start | bytes 147464 | tf_op jit(solution)/shard_map/while/body/eval_jaxpr/ppermute | solution.py:27
  179.1 3.8 %collective-permute-start.3 = (f32[1,2,12,128]{3,0,2,1:T(1,128)S(1)}, f32[1,2,12,128]{3,0,2,1:T(1,128)S(1)}, u32[]{:S(2)}, u32[]{:S(2)}) collective-permute-start(f32[1,2,12,128]{3,0,2,1:T(1,128)S(1)} %slice_bitcast_fusion.19), channel_id=1, source_target_pairs={{1,0},{0,1},{3,2},{2,3},{5,4},{4,5},{7,6},{6,7},{9,8},{8,9},{11,10... | collective-permute-start | bytes 36872 | tf_op jit(solution)/shard_map/while/body/eval_jaxpr/ppermute | solution.py:17
  179.7 3.8 %collective-permute-start.4 = (f32[1,2,12,128]{3,0,2,1:T(1,128)S(1)}, f32[1,2,12,128]{3,0,2,1:T(1,128)S(1)}, u32[]{:S(2)}, u32[]{:S(2)}) collective-permute-start(f32[1,2,12,128]{3,0,2,1:T(1,128)S(1)} %slice_bitcast_fusion.20), channel_id=1, source_target_pairs={{1,0},{0,1},{3,2},{2,3},{5,4},{4,5},{7,6},{6,7},{9,8},{8,9},{11,10... | collective-permute-start | bytes 36872 | tf_op jit(solution)/shard_map/while/body/eval_jaxpr/ppermute | solution.py:17
  183.5 5.9 %collective-permute-start.5 = (f32[1,2,12,128]{3,0,2,1:T(1,128)S(1)}, f32[1,2,12,128]{3,0,2,1:T(1,128)S(1)}, u32[]{:S(2)}, u32[]{:S(2)}) collective-permute-start(f32[1,2,12,128]{3,0,2,1:T(1,128)S(1)} %slice_bitcast_fusion.21), channel_id=1, source_target_pairs={{30,0},{0,2},{2,4},{4,6},{6,8},{8,10},{10,12},{12,14},{14,16},{16,... | collective-permute-start | bytes 36872 | tf_op jit(solution)/shard_map/while/body/eval_jaxpr/ppermute | solution.py:17
  189.4 1.5 collective-permute-start.6
  190.9 3.8 %collective-permute-start.7 = (f32[1,2,1,12,128]{4,0,3,2,1:T(1,128)S(1)}, f32[1,2,1,12,128]{4,0,3,2,1:T(1,128)S(1)}, u32[]{:S(2)}, u32[]{:S(2)}) collective-permute-start(f32[1,2,1,12,128]{4,0,3,2,1:T(1,128)S(1)} %get-tuple-element.2644), channel_id=1, source_target_pairs={{1,0},{0,1},{3,2},{2,3},{5,4},{4,5},{7,6},{6,7},{9,8},{8,9},{11,10... | collective-permute-start | bytes 36872 | tf_op jit(solution)/shard_map/while/body/eval_jaxpr/ppermute | solution.py:28
  192.5 3.8 %collective-permute-start.8 = (f32[1,2,1,12,128]{4,0,3,2,1:T(1,128)S(1)}, f32[1,2,1,12,128]{4,0,3,2,1:T(1,128)S(1)}, u32[]{:S(2)}, u32[]{:S(2)}) collective-permute-start(f32[1,2,1,12,128]{4,0,3,2,1:T(1,128)S(1)} %get-tuple-element.2645), channel_id=1, source_target_pairs={{0,1},{1,0},{2,3},{3,2},{4,5},{5,4},{6,7},{7,6},{8,9},{9,8},{10,11... | collective-permute-start | bytes 36872 | tf_op jit(solution)/shard_map/while/body/eval_jaxpr/ppermute | solution.py:27
  245.5 4.2 %collective-permute-start.9 = (f32[3,2,12,128]{3,0,2,1:T(4,128)S(1)}, f32[3,2,12,128]{3,0,2,1:T(4,128)S(1)}, u32[]{:S(2)}, u32[]{:S(2)}) collective-permute-start(f32[3,2,12,128]{3,0,2,1:T(4,128)S(1)} %get-tuple-element.2738), channel_id=1, source_target_pairs={{1,0},{0,1},{3,2},{2,3},{5,4},{4,5},{7,6},{6,7},{9,8},{8,9},{11,10... | collective-permute-start | bytes 110600 | tf_op jit(solution)/shard_map/while/body/eval_jaxpr/ppermute | solution.py:17
  246.1 4.2 %collective-permute-start.10 = (f32[3,2,12,128]{3,0,2,1:T(4,128)S(1)}, f32[3,2,12,128]{3,0,2,1:T(4,128)S(1)}, u32[]{:S(2)}, u32[]{:S(2)}) collective-permute-start(f32[3,2,12,128]{3,0,2,1:T(4,128)S(1)} %get-tuple-element.2739), channel_id=1, source_target_pairs={{1,0},{0,1},{3,2},{2,3},{5,4},{4,5},{7,6},{6,7},{9,8},{8,9},{11,10... | collective-permute-start | bytes 110600 | tf_op jit(solution)/shard_map/while/body/eval_jaxpr/ppermute | solution.py:17
  250.3 6.3 %collective-permute-start.11 = (f32[3,2,12,128]{3,0,2,1:T(4,128)S(1)}, f32[3,2,12,128]{3,0,2,1:T(4,128)S(1)}, u32[]{:S(2)}, u32[]{:S(2)}) collective-permute-start(f32[3,2,12,128]{3,0,2,1:T(4,128)S(1)} %slice_bitcast_fusion.23), channel_id=1, source_target_pairs={{30,0},{0,2},{2,4},{4,6},{6,8},{8,10},{10,12},{12,14},{14,16},{16,... | collective-permute-start | bytes 110600 | tf_op jit(solution)/shard_map/while/body/eval_jaxpr/ppermute | solution.py:17
  256.8 1.8 collective-permute-start
  258.7 4.6 %collective-permute-start.1 = (f32[4,2,1,12,128]{4,0,3,2,1:T(4,128)S(1)}, f32[4,2,1,12,128]{4,0,3,2,1:T(4,128)S(1)}, u32[]{:S(2)}, u32[]{:S(2)}) collective-permute-start(f32[4,2,1,12,128]{4,0,3,2,1:T(4,128)S(1)} %get-tuple-element.2527), channel_id=1, source_target_pairs={{1,0},{0,1},{3,2},{2,3},{5,4},{4,5},{7,6},{6,7},{9,8},{8,9},{11,10... | collective-permute-start | bytes 147464 | tf_op jit(solution)/shard_map/while/body/eval_jaxpr/ppermute | solution.py:28
  260.3 4.1 %collective-permute-start.2 = (f32[4,2,1,12,128]{4,0,3,2,1:T(4,128)S(1)}, f32[4,2,1,12,128]{4,0,3,2,1:T(4,128)S(1)}, u32[]{:S(2)}, u32[]{:S(2)}) collective-permute-start(f32[4,2,1,12,128]{4,0,3,2,1:T(4,128)S(1)} %get-tuple-element.2528), channel_id=1, source_target_pairs={{0,1},{1,0},{2,3},{3,2},{4,5},{5,4},{6,7},{7,6},{8,9},{9,8},{10,11... | collective-permute-start | bytes 147464 | tf_op jit(solution)/shard_map/while/body/eval_jaxpr/ppermute | solution.py:27
  294.3 3.8 %collective-permute-start.3 = (f32[1,2,12,128]{3,0,2,1:T(1,128)S(1)}, f32[1,2,12,128]{3,0,2,1:T(1,128)S(1)}, u32[]{:S(2)}, u32[]{:S(2)}) collective-permute-start(f32[1,2,12,128]{3,0,2,1:T(1,128)S(1)} %slice_bitcast_fusion.19), channel_id=1, source_target_pairs={{1,0},{0,1},{3,2},{2,3},{5,4},{4,5},{7,6},{6,7},{9,8},{8,9},{11,10... | collective-permute-start | bytes 36872 | tf_op jit(solution)/shard_map/while/body/eval_jaxpr/ppermute | solution.py:17
  294.9 3.8 %collective-permute-start.4 = (f32[1,2,12,128]{3,0,2,1:T(1,128)S(1)}, f32[1,2,12,128]{3,0,2,1:T(1,128)S(1)}, u32[]{:S(2)}, u32[]{:S(2)}) collective-permute-start(f32[1,2,12,128]{3,0,2,1:T(1,128)S(1)} %slice_bitcast_fusion.20), channel_id=1, source_target_pairs={{1,0},{0,1},{3,2},{2,3},{5,4},{4,5},{7,6},{6,7},{9,8},{8,9},{11,10... | collective-permute-start | bytes 36872 | tf_op jit(solution)/shard_map/while/body/eval_jaxpr/ppermute | solution.py:17
  298.7 5.9 %collective-permute-start.5 = (f32[1,2,12,128]{3,0,2,1:T(1,128)S(1)}, f32[1,2,12,128]{3,0,2,1:T(1,128)S(1)}, u32[]{:S(2)}, u32[]{:S(2)}) collective-permute-start(f32[1,2,12,128]{3,0,2,1:T(1,128)S(1)} %slice_bitcast_fusion.21), channel_id=1, source_target_pairs={{30,0},{0,2},{2,4},{4,6},{6,8},{8,10},{10,12},{12,14},{14,16},{16,... | collective-permute-start | bytes 36872 | tf_op jit(solution)/shard_map/while/body/eval_jaxpr/ppermute | solution.py:17
  304.6 1.5 collective-permute-start.6
  306.1 3.8 %collective-permute-start.7 = (f32[1,2,1,12,128]{4,0,3,2,1:T(1,128)S(1)}, f32[1,2,1,12,128]{4,0,3,2,1:T(1,128)S(1)}, u32[]{:S(2)}, u32[]{:S(2)}) collective-permute-start(f32[1,2,1,12,128]{4,0,3,2,1:T(1,128)S(1)} %get-tuple-element.2644), channel_id=1, source_target_pairs={{1,0},{0,1},{3,2},{2,3},{5,4},{4,5},{7,6},{6,7},{9,8},{8,9},{11,10... | collective-permute-start | bytes 36872 | tf_op jit(solution)/shard_map/while/body/eval_jaxpr/ppermute | solution.py:28
  307.7 3.8 %collective-permute-start.8 = (f32[1,2,1,12,128]{4,0,3,2,1:T(1,128)S(1)}, f32[1,2,1,12,128]{4,0,3,2,1:T(1,128)S(1)}, u32[]{:S(2)}, u32[]{:S(2)}) collective-permute-start(f32[1,2,1,12,128]{4,0,3,2,1:T(1,128)S(1)} %get-tuple-element.2645), channel_id=1, source_target_pairs={{0,1},{1,0},{2,3},{3,2},{4,5},{5,4},{6,7},{7,6},{8,9},{9,8},{10,11... | collective-permute-start | bytes 36872 | tf_op jit(solution)/shard_map/while/body/eval_jaxpr/ppermute | solution.py:27
  360.8 4.2 %collective-permute-start.9 = (f32[3,2,12,128]{3,0,2,1:T(4,128)S(1)}, f32[3,2,12,128]{3,0,2,1:T(4,128)S(1)}, u32[]{:S(2)}, u32[]{:S(2)}) collective-permute-start(f32[3,2,12,128]{3,0,2,1:T(4,128)S(1)} %get-tuple-element.2738), channel_id=1, source_target_pairs={{1,0},{0,1},{3,2},{2,3},{5,4},{4,5},{7,6},{6,7},{9,8},{8,9},{11,10... | collective-permute-start | bytes 110600 | tf_op jit(solution)/shard_map/while/body/eval_jaxpr/ppermute | solution.py:17
  361.4 4.2 %collective-permute-start.10 = (f32[3,2,12,128]{3,0,2,1:T(4,128)S(1)}, f32[3,2,12,128]{3,0,2,1:T(4,128)S(1)}, u32[]{:S(2)}, u32[]{:S(2)}) collective-permute-start(f32[3,2,12,128]{3,0,2,1:T(4,128)S(1)} %get-tuple-element.2739), channel_id=1, source_target_pairs={{1,0},{0,1},{3,2},{2,3},{5,4},{4,5},{7,6},{6,7},{9,8},{8,9},{11,10... | collective-permute-start | bytes 110600 | tf_op jit(solution)/shard_map/while/body/eval_jaxpr/ppermute | solution.py:17
  365.6 6.3 %collective-permute-start.11 = (f32[3,2,12,128]{3,0,2,1:T(4,128)S(1)}, f32[3,2,12,128]{3,0,2,1:T(4,128)S(1)}, u32[]{:S(2)}, u32[]{:S(2)}) collective-permute-start(f32[3,2,12,128]{3,0,2,1:T(4,128)S(1)} %slice_bitcast_fusion.23), channel_id=1, source_target_pairs={{30,0},{0,2},{2,4},{4,6},{6,8},{8,10},{10,12},{12,14},{14,16},{16,... | collective-permute-start | bytes 110600 | tf_op jit(solution)/shard_map/while/body/eval_jaxpr/ppermute | solution.py:17
where the time goes:
time: 374 us
  other arithmetic  212 us (57%)
  waiting for transfers between devices  76.8 us (21%)
  local copies, waits for them, and re-layouts  32 us (9%)
  starting transfers between devices  32 us (9%)
  loops' own time  17.5 us (5%)
    reduce_sum x21, other arithmetic, forces_once(): jnp.sum(coupling * parts[component], axis=-2)  129 us
    reduce_sum x15, other arithmetic, forces_once(): gathered = add_block(gathered, offset, jnp.sum(term, axis=-2)[None])  60.2 us
    ppermute x24, waiting for transfers between devices, passed_along(): return lax.ppermute(block, axis, route)  58.7 us
    scatter-add x74, local copies, waits for them, and re-layouts, add_block(): return buffer.at[:, first:first + shape[1], second:second + shape[2], thi...  20.9 us
    ppermute x24, starting transfers between devices, passed_along(): return lax.ppermute(block, axis, route)  19.3 us
    another operation x1, loops' own time, shards(): lax.fori_loop(0, STEPS, verlet_step, (positions, velocities, pushed))  17.5 us
    ppermute x6, waiting for transfers between devices, with_halo(): after = lax.ppermute(first, axis, down)  9.81 us
    add x68, other arithmetic, add_block(): return buffer.at[:, first:first + shape[1], second:second + shape[2], thi...  9.2 us
  transfers between devices with their start and end apart: 36, of which 36 were waited for; matrix products, arithmetic and copies ran while one was open for 1% of the time, Pallas kernels for 0%

commit v1 on v0

v1 whole, which is shorter than its diff:
```python
import functools

import jax
import jax.numpy as jnp
from jax import lax
from jax.experimental import pallas as pl
from jax.experimental.pallas import tpu as pltpu
from jax.sharding import PartitionSpec as P

STEPS = 2
TIME_STEP = 0.05
DENSITY_SCALE = 0.0625
PAIR_SCALE = 0.0625
ABSENT = 1.0e6

FEATURES = 32
ROWS = 16
NEAR = (-1, 0, 1)
MESH = pl.DeviceIdType.MESH


def split3(value):
    high = value.astype(jnp.bfloat16).astype(jnp.float32)
    rest = value - high
    middle = rest.astype(jnp.bfloat16).astype(jnp.float32)
    return high, middle, rest - middle


def split2(value):
    high = value.astype(jnp.bfloat16).astype(jnp.float32)
    return high, value - high


def directions():
    return [(dx, dy) for dx in NEAR for dy in NEAR if (dx, dy) != (0, 0)]


def neighbour(sizes, dx, dy):
    gx = lax.rem(lax.axis_index("gx") + sizes[0] + dx, sizes[0])
    gy = lax.rem(lax.axis_index("gy") + sizes[1] + dy, sizes[1])
    return (gx, gy)


def exchange(buffer, sizes, columns, send_sem, recv_sem):
    copies = []
    for slot, (dx, dy) in enumerate(directions()):
        first, count, landing = 1, columns, 1
        if dy == 1:
            first, count, landing = columns, 1, 0
        if dy == -1:
            first, count, landing = 1, 1, columns + 1
        copies.append(
            pltpu.make_async_remote_copy(
                src_ref=buffer.at[1, pl.ds(first, count)],
                dst_ref=buffer.at[1 - dx, pl.ds(landing, count)],
                send_sem=send_sem.at[slot],
                recv_sem=recv_sem.at[slot],
                device_id=neighbour(sizes, dx, dy),
                device_id_type=MESH,
            )
        )
    for copy in copies:
        copy.start()
    return copies


def kernel(
    sizes, columns, depth, slots,
    pos_in, vel_in, mask_in, pos_out, vel_out, force_out,
    places, slopes, frame, own_rows, near_rows, near_cols, self_rows, blocks,
    sum_rows, sums, slope_rows, slope_sums, held, cubes, partial,
    place_send, place_recv, slope_send, slope_recv,
):
    wide = columns + 2
    f32, bf16 = jnp.float32, jnp.bfloat16
    cells = columns * depth

    barrier = pltpu.get_barrier_semaphore()
    greeted = [(dx, dy) for dx, dy in directions() if not (sizes[1] == 2 and dy == -1)]
    for dx, dy in greeted:
        pl.semaphore_signal(barrier, inc=1, device_id=neighbour(sizes, dx, dy), device_id_type=MESH)
    pl.semaphore_wait(barrier, len(greeted))

    for component in range(3):
        for column in range(columns):
            places[1, 1 + column, component] = pos_in[component, column]
            vel_out[component, column] = vel_in[component, column]
    for column in range(columns):
        places[1, 1 + column, 3] = mask_in[column]

    near_rows[...] = jnp.zeros_like(near_rows)
    self_rows[...] = jnp.zeros_like(self_rows)
    blocks[...] = jnp.zeros_like(blocks)
    sum_rows[...] = jnp.zeros_like(sum_rows)
    slope_rows[...] = jnp.zeros_like(slope_rows)
    own_rows[...] = jnp.zeros_like(own_rows)
    ones = jnp.ones((depth, slots), f32)

    def put(ref, index, row, stride, value):
        ref[index + (pl.ds(row, depth, stride=stride), slice(None))] = value

    for v in range(wide):
        for u in range(3):
            for row in (21, 22, 23):
                put(near_rows, (v,), u * FEATURES + row, 128, ones)
            put(sum_rows, (u, v), 3, ROWS, ones)
            put(sum_rows, (u, v), 14, ROWS, ones)
    for column in range(columns):
        put(own_rows, (column,), 3, 8, ones)
        for r in range(3):
            for row in (18, 19, 20):
                put(self_rows, (r, column), row, FEATURES, ones)

    def build_column(u, v):
        mask = places[u, v, 3]
        spots = (
            places[u, v, 0] + (u - 1.5),
            places[u, v, 1] + (v - 1.0 - 0.5 * columns),
            places[u, v, 2] - 0.5,
        )
        norm = jnp.where(mask > 0.0, spots[0] * spots[0] + spots[1] * spots[1] + spots[2] * spots[2], ABSENT)
        base = u * FEATURES
        for c in range(3):
            frame[u, v, c] = spots[c]
            h, m, l = split3(spots[c])
            for place, value in enumerate((h, h, m, h, l, m)):
                put(near_rows, (v,), base + 6 * c + place, 128, value)
            put(sum_rows, (u, v), c, ROWS, h)
            put(sum_rows, (u, v), 4 + c, ROWS, m)
            put(sum_rows, (u, v), 8 + c, ROWS, l)
        for place, value in enumerate(split3(-norm)):
            put(near_rows, (v,), base + 18 + place, 128, value)

    def build_own(column):
        v = column + 1
        spots = (
            places[1, v, 0] - 0.5,
            places[1, v, 1] + (v - 1.0 - 0.5 * columns),
            places[1, v, 2] - 0.5,
        )
        for c in range(3):
            put(own_rows, (column,), c, 8, spots[c])
        for r in range(3):
            moved = (spots[0], spots[1], spots[2] - (r - 1.0))
            norm = moved[0] * moved[0] + moved[1] * moved[1] + moved[2] * moved[2]
            for c in range(3):
                h, m, l = split3(2.0 * moved[c])
                for place, value in enumerate((h, m, h, l, h, m)):
                    put(self_rows, (r, column), 6 * c + place, FEATURES, value)
            for place, value in enumerate(split3(1.0 - norm)):
                put(self_rows, (r, column), 21 + place, FEATURES, value)

    def build_slopes(u, v):
        near = slopes[u, v]
        for c in range(3):
            h, m = split2(near * frame[u, v, c])
            put(slope_rows, (u, v), c, ROWS, h)
            put(slope_rows, (u, v), 4 + c, ROWS, m)
        h, m = split2(near)
        put(slope_rows, (u, v), 3, ROWS, h)
        put(slope_rows, (u, v), 7, ROWS, m)
        put(slope_rows, (u, v), 10, ROWS, h)
        put(slope_rows, (u, v), 14, ROWS, m)

    row_ids = lax.broadcasted_iota(jnp.int32, (ROWS, slots), 0)

    def scaled(first):
        return [jnp.where(row_ids >= first, float(r), 1.0).astype(bf16) for r in NEAR]

    def rows_of(ref, u, column, layers, scales):
        parts = []
        for q in range(3):
            for r in range(3):
                start = pl.multiple_of(layers[r] * ROWS, ROWS)
                parts.append(ref[u, column + q, pl.ds(start, ROWS), :] * scales[r])
        return jnp.concatenate(parts, axis=1)

    def folded(total):
        both = total[:, :slots] + total[:, slots:]
        half = both[:8] + both[8:]
        return half[:4] + half[4:]

    def spread(total, own):
        return total - own[:4] * total[3:4]

    def layers_of(z):
        return [lax.rem(z + r + depth, depth) for r in NEAR]

    def first_pass(cell, carry):
        column, z = lax.div(cell, depth), lax.rem(cell, depth)
        layers = layers_of(z)
        for r in range(3):
            start = pl.multiple_of(z * FEATURES, FEATURES)
            block = self_rows[r, column, pl.ds(start, FEATURES), :].astype(bf16)
            for u in range(3):
                blocks[r, pl.ds(u * FEATURES, FEATURES), pl.ds(u * slots, slots)] = block
        density = jnp.zeros((8, slots), f32)
        for q in range(3):
            for r in range(3):
                start = pl.multiple_of(layers[r] * 128, 128)
                near = near_cols[column + q, pl.ds(start, slots), :]
                for u in range(3):
                    reach = jnp.dot(near, blocks[r, :, u * slots:(u + 1) * slots], preferred_element_type=f32)
                    reach = jnp.maximum(reach, 0.0)
                    square = reach * reach
                    density = density + jnp.sum(square.reshape(slots // 8, 8, slots), axis=0)
                    cube = square * reach
                    high = reach.astype(bf16)
                    low = (reach - high.astype(f32)).astype(bf16)
                    rows = pl.ds((q * 3 + r) * slots, slots)
                    held[cell * 3 + u, rows, pl.ds(0, slots)] = high
                    held[cell * 3 + u, rows, pl.ds(slots, slots)] = low
                    high = cube.astype(bf16)
                    low = (cube - high.astype(f32)).astype(bf16)
                    cubes[u, rows, pl.ds(0, slots)] = high
                    cubes[u, rows, pl.ds(slots, slots)] = low
        own = own_rows[column, pl.ds(pl.multiple_of(z * 8, 8), 8), :]
        present = places[1, column + 1, 3, pl.ds(z, 1), :]
        density = DENSITY_SCALE * (jnp.sum(density, axis=0, keepdims=True) - present)
        slope = 2.0 * DENSITY_SCALE * 2.0 * 0.5 / jnp.sqrt(1.0 + density)
        slopes[1, column + 1, pl.ds(z, 1), :] = slope
        scales = scaled(12)
        linear = jnp.zeros((ROWS, 2 * slots), f32)
        cubic = jnp.zeros((ROWS, 2 * slots), f32)
        for u in range(3):
            lhs = rows_of(sums, u, column, layers, scales)
            linear = linear + jnp.dot(lhs, held[cell * 3 + u], preferred_element_type=f32)
            cubic = cubic + jnp.dot(lhs, cubes[u], preferred_element_type=f32)
        force = slope * spread(folded(linear), own) - (8.0 * PAIR_SCALE) * spread(folded(cubic), own)
        partial[column, pl.ds(pl.multiple_of(z * 8, 8), 4), :] = force
        return carry

    def second_pass(cell, carry):
        column, z = lax.div(cell, depth), lax.rem(cell, depth)
        layers = layers_of(z)
        own = own_rows[column, pl.ds(pl.multiple_of(z * 8, 8), 8), :]
        scales = scaled(8)
        total = jnp.zeros((ROWS, 2 * slots), f32)
        for u in range(3):
            lhs = rows_of(slope_sums, u, column, layers, scales)
            total = total + jnp.dot(lhs, held[cell * 3 + u], preferred_element_type=f32)
        where = pl.ds(pl.multiple_of(z * 8, 8), 4)
        partial[column, where, :] = partial[column, where, :] + spread(folded(total), own)
        return carry

    def turned(index, carry):
        v, z = lax.div(index, depth), lax.rem(index, depth)
        rows = pl.ds(pl.multiple_of(z * 128, 128), 128)
        near_cols[v, rows, :] = near_rows[v, rows, :].T.astype(bf16)
        return carry

    def evaluate(step, carry):
        copies = exchange(places, sizes, columns, place_send, place_recv)
        for column in range(columns):
            build_own(column)
            build_column(1, column + 1)
        for copy in copies:
            copy.wait()
        for u in range(3):
            for v in range(wide):
                if u != 1 or v in (0, wide - 1):
                    build_column(u, v)
        for u in range(3):
            for v in range(wide):
                sums[u, v] = sum_rows[u, v].astype(bf16)
        lax.fori_loop(0, wide * depth, turned, 0)
        lax.fori_loop(0, cells, first_pass, 0)
        copies = exchange(slopes, sizes, columns, slope_send, slope_recv)
        for copy in copies:
            copy.wait()
        for u in range(3):
            for v in range(wide):
                build_slopes(u, v)
                slope_sums[u, v] = slope_rows[u, v].astype(bf16)
        lax.fori_loop(0, cells, second_pass, 0)
        begin = jnp.where(step > 0, 0.5 * TIME_STEP, 0.0)
        end = jnp.where(step < STEPS, 0.5 * TIME_STEP, 0.0)
        drift = jnp.where(step < STEPS, TIME_STEP, 0.0)
        for column in range(columns):
            for c in range(3):
                force = partial[column, pl.ds(c, depth, stride=8), :] * places[1, column + 1, 3]
                force_out[c, column] = force
                speed = (vel_out[c, column] + begin * force) + end * force
                vel_out[c, column] = speed
                places[1, column + 1, c] = places[1, column + 1, c] + drift * speed
        return carry

    lax.fori_loop(0, STEPS + 1, evaluate, 0)
    for c in range(3):
        for column in range(columns):
            pos_out[c, column] = places[1, column + 1, c]


def shards(sizes, positions, velocities, counts):
    _, _, columns, depth, slots = positions.shape
    filled = lax.broadcasted_iota(jnp.int32, (columns, depth, slots), 2) < counts.reshape(columns, depth, 1)
    shape = (3, columns, depth, slots)
    wide = columns + 2
    cells = columns * depth
    f32, bf16 = jnp.float32, jnp.bfloat16
    vmem = pl.BlockSpec(memory_space=pltpu.VMEM)
    outs = pl.pallas_call(
        functools.partial(kernel, sizes, columns, depth, slots),
        out_shape=[jax.ShapeDtypeStruct(shape, f32)] * 3,
        in_specs=[vmem] * 3,
        out_specs=[vmem] * 3,
        scratch_shapes=[
            pltpu.VMEM((3, wide, 4, depth, slots), f32),
            pltpu.VMEM((3, wide, depth, slots), f32),
            pltpu.VMEM((3, wide, 3, depth, slots), f32),
            pltpu.VMEM((columns, depth * 8, slots), f32),
            pltpu.VMEM((wide, depth * 128, slots), f32),
            pltpu.VMEM((wide, depth * slots, 128), bf16),
            pltpu.VMEM((3, columns, depth * FEATURES, slots), f32),
            pltpu.VMEM((3, 128, 3 * slots), bf16),
            pltpu.VMEM((3, wide, depth * ROWS, slots), f32),
            pltpu.VMEM((3, wide, depth * ROWS, slots), bf16),
            pltpu.VMEM((3, wide, depth * ROWS, slots), f32),
            pltpu.VMEM((3, wide, depth * ROWS, slots), bf16),
            pltpu.VMEM((cells * 3, 9 * slots, 2 * slots), bf16),
            pltpu.VMEM((3, 9 * slots, 2 * slots), bf16),
            pltpu.VMEM((columns, depth * 8, slots), f32),
            pltpu.SemaphoreType.DMA((8,)),
            pltpu.SemaphoreType.DMA((8,)),
            pltpu.SemaphoreType.DMA((8,)),
            pltpu.SemaphoreType.DMA((8,)),
        ],
        compiler_params=pltpu.CompilerParams(
            collective_id=0, has_side_effects=True, vmem_limit_bytes=60 * 1024 * 1024
        ),
        name="verlet",
    )(positions.reshape(shape), velocities.reshape(shape), filled.astype(f32))
    return tuple(out.reshape(positions.shape) for out in outs)


def solution(mesh):
    grid = P(None, "gx", "gy", None, None)
    sizes = (mesh.shape["gx"], mesh.shape["gy"])
    return jax.shard_map(
        functools.partial(shards, sizes),
        mesh=mesh,
        in_specs=(grid, grid, P("gx", "gy", None)),
        out_specs=(grid, grid, grid),
        check_vma=False,
    )
```

time: 374 us -> 189 us (0.51)
  other arithmetic: 212 us -> 0.68 us
  Pallas kernels: 0 us -> 183 us
  waiting for transfers between devices: 76.8 us -> 0 us
  starting transfers between devices: 32 us -> 0 us
  local copies, waits for them, and re-layouts: 32 us -> 4.98 us
  loops' own time: 17.5 us -> 0 us
    reduce_sum x36 -> x0, other arithmetic: 190 us -> none  [the longest x21 129 us: forces_once(): jnp.sum(coupling * parts[component], axis=-2)]
    pallas_call x0 -> x1, Pallas kernels: none -> 183 us  [shards(): pl.pallas_call(functools.partial(kernel, sizes, columns, depth, slots), o...]
    ppermute x36 -> x0, waiting for transfers between devices: 76.8 us -> none  [the longest x24 58.7 us: passed_along(): return lax.ppermute(block, axis, route)]
    ppermute x36 -> x0, starting transfers between devices: 32 us -> none  [the longest x24 19.3 us: passed_along(): return lax.ppermute(block, axis, route)]
    scatter-add x81 -> x0, local copies, waits for them, and re-layouts: 21.5 us -> none  [the longest x74 20.9 us: add_block(): return buffer.at[:, first:first + shape[1], second:second + shape[2], thi...]
    another operation x1 -> x0, loops' own time: 17.5 us -> none  [shards(): lax.fori_loop(0, STEPS, verlet_step, (positions, velocities, pushed))]
    add x101 -> x0, other arithmetic: 10.3 us -> none  [the longest x68 9.2 us: add_block(): return buffer.at[:, first:first + shape[1], second:second + shape[2], thi...]
    scatter-add x110 -> x0, other arithmetic: 8.68 us -> none  [the longest x88 8.31 us: add_block(): return buffer.at[:, first:first + shape[1], second:second + shape[2], thi...]
  transfers between devices with their start and end apart: 36 -> 0, of which waited for: 36 -> 0; matrix products, arithmetic and copies ran while one was open for 1% -> 0% of each run, Pallas kernels for 0% -> 0%
where the time goes in v1:
time: 189 us
  Pallas kernels  183 us (97%)
  local copies, waits for them, and re-layouts  4.98 us (3%)
    pallas_call x1, Pallas kernels, shards(): pl.pallas_call(functools.partial(kernel, sizes, columns, depth, slots), o...  183 us

profile of v1, /device:TPU:0, one launch (start us, length us, event | category | flops | bytes accessed | tf_op | source)
XLA Modules:
  0.0 188.9 jit_solution(758215712341398713)
XLA Ops:
  0.6 0.0 copy-start.2
  0.6 0.7 copy-done.2
  1.3 0.7 fusion.mask_in
  2.0 1.4 copy_bitcast_fusion
  3.4 182.6 %verlet.1 = (f32[3,2,12,128]{3,2,1,0:T(8,128)}, f32[3,2,12,128]{3,2,1,0:T(8,128)}, f32[3,2,12,128]{3,2,1,0:T(8,128)}) custom-call(f32[3,2,12,128]{3,2,1,0:T(8,128)} %get-tuple-element.13.pos_in, f32[3,2,12,128]{3,2,1,0:T(8,128)} %get-tuple-element.12.vel_in, f32[2,12,128]{2,1,0:T(8,128)} %fusion.mask_in), custom_call_target="tpu_custom_call" | custom-call | tf_op jit(solution)/shard_map/verlet/pallas_call | solution.py:302
  186.0 0.0 copy-start.1
  186.0 1.4 copy.8
  187.5 0.0 copy-start
  187.5 0.0 copy-done.1
  187.5 0.6 copy.9
  188.1 0.2 copy-done
  188.3 0.6 copy.10
Async XLA Ops:
  0.6 0.7 copy-start.2
  186.0 1.5 copy-start.1
  187.5 0.8 copy-start

commit v2 on v1

v2 whole, which is shorter than its diff:
```python
import functools

import jax
import jax.numpy as jnp
from jax import lax
from jax.experimental import pallas as pl
from jax.experimental.pallas import tpu as pltpu
from jax.sharding import PartitionSpec as P

STEPS = 2
TIME_STEP = 0.05
DENSITY_SCALE = 0.0625
PAIR_SCALE = 0.0625
ABSENT = 1.0e6

FEATURES = 32
TALL = 32
NEAR = (-1, 0, 1)
MESH = pl.DeviceIdType.MESH


def split3(value):
    high = value.astype(jnp.bfloat16).astype(jnp.float32)
    rest = value - high
    middle = rest.astype(jnp.bfloat16).astype(jnp.float32)
    return high, middle, rest - middle


def directions():
    return [(dx, dy) for dx in NEAR for dy in NEAR if (dx, dy) != (0, 0)]


def neighbour(sizes, dx, dy):
    gx = lax.rem(lax.axis_index("gx") + sizes[0] + dx, sizes[0])
    gy = lax.rem(lax.axis_index("gy") + sizes[1] + dy, sizes[1])
    return (gx, gy)


def exchange(buffer, sizes, columns, send_sem, recv_sem):
    copies = []
    for slot, (dx, dy) in enumerate(directions()):
        first, count, landing = 1, columns, 1
        if dy == 1:
            first, count, landing = columns, 1, 0
        if dy == -1:
            first, count, landing = 1, 1, columns + 1
        copies.append(
            pltpu.make_async_remote_copy(
                src_ref=buffer.at[1, pl.ds(first, count)],
                dst_ref=buffer.at[1 - dx, pl.ds(landing, count)],
                send_sem=send_sem.at[slot],
                recv_sem=recv_sem.at[slot],
                device_id=neighbour(sizes, dx, dy),
                device_id_type=MESH,
            )
        )
    for copy in copies:
        copy.start()
    return copies


def kernel(
    sizes, columns, depth, slots,
    pos_in, vel_in, mask_in, pos_out, vel_out, force_out,
    places, slopes, frame, near_rows, near_cols, self_rows, self_cols,
    own_slopes, held, totals, partial,
    place_send, place_recv, slope_send, slope_recv,
):
    wide = columns + 2
    f32, bf16 = jnp.float32, jnp.bfloat16
    cells = columns * depth

    barrier = pltpu.get_barrier_semaphore()
    greeted = [(dx, dy) for dx, dy in directions() if not (sizes[1] == 2 and dy == -1)]
    for dx, dy in greeted:
        pl.semaphore_signal(barrier, inc=1, device_id=neighbour(sizes, dx, dy), device_id_type=MESH)
    pl.semaphore_wait(barrier, len(greeted))

    for component in range(3):
        for column in range(columns):
            places[1, 1 + column, component] = pos_in[component, column]
            vel_out[component, column] = vel_in[component, column]
    for column in range(columns):
        places[1, 1 + column, 3] = mask_in[column]

    near_rows[...] = jnp.zeros_like(near_rows)
    self_rows[...] = jnp.zeros_like(self_rows)
    frame[...] = jnp.zeros_like(frame)
    ones = jnp.ones((depth, slots), f32)

    def put(ref, index, row, stride, value):
        ref[index + (pl.ds(row, depth, stride=stride), slice(None))] = value

    for v in range(wide):
        for u in range(3):
            for row in (21, 22, 23):
                put(near_rows, (u, v), row, FEATURES, ones)
    for column in range(columns):
        for r in range(3):
            for row in (18, 19, 20):
                put(self_rows, (r, column), row, FEATURES, ones)

    def build_column(u, v):
        mask = places[u, v, 3]
        spots = (
            places[u, v, 0] + (u - 1.5),
            places[u, v, 1] + (v - 1.0 - 0.5 * columns),
            places[u, v, 2] - 0.5,
        )
        norm = jnp.where(mask > 0.0, spots[0] * spots[0] + spots[1] * spots[1] + spots[2] * spots[2], ABSENT)
        for c in range(3):
            h, m, l = split3(spots[c])
            for place, value in enumerate((h, h, m, h, l, m)):
                put(near_rows, (u, v), 6 * c + place, FEATURES, value)
        for place, value in enumerate(split3(-norm)):
            put(near_rows, (u, v), 18 + place, FEATURES, value)
        for row, value in enumerate((spots[0], spots[1], spots[2] - 1.0, spots[2], spots[2] + 1.0)):
            put(frame, (u, v), row, 8, value)
        near_cols[v, :, u * slots:(u + 1) * slots] = near_rows[u, v].astype(bf16)

    def build_own(column):
        v = column + 1
        spots = (
            places[1, v, 0] - 0.5,
            places[1, v, 1] + (v - 1.0 - 0.5 * columns),
            places[1, v, 2] - 0.5,
        )
        for r in range(3):
            moved = (spots[0], spots[1], spots[2] - (r - 1.0))
            norm = moved[0] * moved[0] + moved[1] * moved[1] + moved[2] * moved[2]
            for c in range(3):
                h, m, l = split3(2.0 * moved[c])
                for place, value in enumerate((h, m, h, l, h, m)):
                    put(self_rows, (r, column), 6 * c + place, FEATURES, value)
            for place, value in enumerate(split3(1.0 - norm)):
                put(self_rows, (r, column), 21 + place, FEATURES, value)

    def turned(cell, carry):
        column, z = lax.div(cell, depth), lax.rem(cell, depth)
        rows = pl.ds(pl.multiple_of(z * FEATURES, FEATURES), FEATURES)
        for r in range(3):
            self_cols[r, cell] = self_rows[r, column, rows, :].T.astype(bf16)
        return carry

    def layers_of(z):
        return [lax.rem(z + r + depth, depth) for r in NEAR]

    def first_pass(cell, carry):
        column, z = lax.div(cell, depth), lax.rem(cell, depth)
        layers = layers_of(z)
        density = jnp.zeros((slots, slots), f32)
        for r in range(3):
            start = pl.multiple_of(layers[r] * FEATURES, FEATURES)
            for q in range(3):
                near = near_cols[column + q, pl.ds(start, FEATURES), :]
                reach = jnp.maximum(jnp.dot(self_cols[r, cell], near, preferred_element_type=f32), 0.0)
                for u in range(3):
                    part = reach[:, u * slots:(u + 1) * slots]
                    held[cell, (q * 3 + r) * 3 + u] = part
                    density = density + part * part
        present = places[1, column + 1, 3, pl.ds(z, 1), :]
        density = DENSITY_SCALE * (jnp.sum(density.T, axis=0, keepdims=True) - present)
        slope = DENSITY_SCALE / (4.0 * PAIR_SCALE) / jnp.sqrt(1.0 + density)
        slopes[1, column + 1, pl.ds(z, 1), :] = slope
        own_slopes[cell] = jnp.broadcast_to(slope, (slots, slots)).T
        return carry

    def second_pass(cell, carry):
        column, z = lax.div(cell, depth), lax.rem(cell, depth)
        layers = layers_of(z)
        for block in range(slots // TALL):
            rows = pl.ds(block * TALL, TALL)
            own = own_slopes[cell, rows, :]
            sums = [jnp.zeros((TALL, slots), f32)] * 4
            for q in range(3):
                for r in range(3):
                    for u in range(3):
                        at = [frame[u, column + q, pl.ds(layers[r] * 8 + row, 1), :] for row in (0, 1, 2 + r, 5)]
                        reach = held[cell, (q * 3 + r) * 3 + u, rows, :]
                        pull = reach * ((own + at[3]) - reach * reach)
                        for c in range(3):
                            sums[c] = sums[c] + pull * at[c]
                        sums[3] = sums[3] + pull
            for c in range(4):
                totals[c, rows, :] = sums[c]
        summed = [jnp.sum(totals[c].T, axis=0, keepdims=True) for c in range(4)]
        for c, row in enumerate((0, 1, 3)):
            own = frame[1, column + 1, pl.ds(z * 8 + row, 1), :]
            partial[column, pl.ds(z * 8 + c, 1), :] = (8.0 * PAIR_SCALE) * (summed[c] - own * summed[3])
        return carry

    def evaluate(step, carry):
        copies = exchange(places, sizes, columns, place_send, place_recv)
        for column in range(columns):
            build_own(column)
            build_column(1, column + 1)
        lax.fori_loop(0, cells, turned, 0)
        for copy in copies:
            copy.wait()
        for u in range(3):
            for v in range(wide):
                if u != 1 or v in (0, wide - 1):
                    build_column(u, v)
        lax.fori_loop(0, cells, first_pass, 0)
        copies = exchange(slopes, sizes, columns, slope_send, slope_recv)
        for copy in copies:
            copy.wait()
        for u in range(3):
            for v in range(wide):
                put(frame, (u, v), 5, 8, slopes[u, v])
        lax.fori_loop(0, cells, second_pass, 0)
        begin = jnp.where(step > 0, 0.5 * TIME_STEP, 0.0)
        end = jnp.where(step < STEPS, 0.5 * TIME_STEP, 0.0)
        drift = jnp.where(step < STEPS, TIME_STEP, 0.0)
        for column in range(columns):
            for c in range(3):
                force = partial[column, pl.ds(c, depth, stride=8), :] * places[1, column + 1, 3]
                force_out[c, column] = force
                speed = (vel_out[c, column] + begin * force) + end * force
                vel_out[c, column] = speed
                places[1, column + 1, c] = places[1, column + 1, c] + drift * speed
        return carry

    lax.fori_loop(0, STEPS + 1, evaluate, 0)
    for c in range(3):
        for column in range(columns):
            pos_out[c, column] = places[1, column + 1, c]


def shards(sizes, positions, velocities, counts):
    _, _, columns, depth, slots = positions.shape
    filled = lax.broadcasted_iota(jnp.int32, (columns, depth, slots), 2) < counts.reshape(columns, depth, 1)
    shape = (3, columns, depth, slots)
    wide = columns + 2
    cells = columns * depth
    f32, bf16 = jnp.float32, jnp.bfloat16
    vmem = pl.BlockSpec(memory_space=pltpu.VMEM)
    outs = pl.pallas_call(
        functools.partial(kernel, sizes, columns, depth, slots),
        out_shape=[jax.ShapeDtypeStruct(shape, f32)] * 3,
        in_specs=[vmem] * 3,
        out_specs=[vmem] * 3,
        scratch_shapes=[
            pltpu.VMEM((3, wide, 4, depth, slots), f32),
            pltpu.VMEM((3, wide, depth, slots), f32),
            pltpu.VMEM((3, wide, depth * 8, slots), f32),
            pltpu.VMEM((3, wide, depth * FEATURES, slots), f32),
            pltpu.VMEM((wide, depth * FEATURES, 3 * slots), bf16),
            pltpu.VMEM((3, columns, depth * FEATURES, slots), f32),
            pltpu.VMEM((3, cells, slots, FEATURES), bf16),
            pltpu.VMEM((cells, slots, slots), f32),
            pltpu.VMEM((cells, 27, slots, slots), f32),
            pltpu.VMEM((4, slots, slots), f32),
            pltpu.VMEM((columns, depth * 8, slots), f32),
            pltpu.SemaphoreType.DMA((8,)),
            pltpu.SemaphoreType.DMA((8,)),
            pltpu.SemaphoreType.DMA((8,)),
            pltpu.SemaphoreType.DMA((8,)),
        ],
        compiler_params=pltpu.CompilerParams(
            collective_id=0, has_side_effects=True, vmem_limit_bytes=60 * 1024 * 1024
        ),
        name="verlet",
    )(positions.reshape(shape), velocities.reshape(shape), filled.astype(f32))
    return tuple(out.reshape(positions.shape) for out in outs)


def solution(mesh):
    grid = P(None, "gx", "gy", None, None)
    sizes = (mesh.shape["gx"], mesh.shape["gy"])
    return jax.shard_map(
        functools.partial(shards, sizes),
        mesh=mesh,
        in_specs=(grid, grid, P("gx", "gy", None)),
        out_specs=(grid, grid, grid),
        check_vma=False,
    )
```

time: 189 us -> 151 us (0.80)
  Pallas kernels: 183 us -> 145 us
    pallas_call x1, Pallas kernels: 183 us -> 145 us  [shards(): pl.pallas_call(functools.partial(kernel, sizes, columns, depth, slots), o...]
where the time goes in v2:
time: 151 us
  Pallas kernels  145 us (96%)
  local copies, waits for them, and re-layouts  4.98 us (3%)
    pallas_call x1, Pallas kernels, shards(): pl.pallas_call(functools.partial(kernel, sizes, columns, depth, slots), o...  145 us
    unnamed x9, local copies, waits for them, and re-layouts  3.55 us

profile of v2, /device:TPU:0, one launch (start us, length us, event | category | flops | bytes accessed | tf_op | source)
XLA Modules:
  0.0 150.9 jit_solution(14417316136332743652)
XLA Ops:
  0.6 0.0 copy-start.2
  0.6 0.7 copy-done.2
  1.3 0.7 fusion.mask_in
  2.0 1.4 copy_bitcast_fusion
  3.4 144.6 %verlet.1 = (f32[3,2,12,128]{3,2,1,0:T(8,128)}, f32[3,2,12,128]{3,2,1,0:T(8,128)}, f32[3,2,12,128]{3,2,1,0:T(8,128)}) custom-call(f32[3,2,12,128]{3,2,1,0:T(8,128)} %get-tuple-element.13.pos_in, f32[3,2,12,128]{3,2,1,0:T(8,128)} %get-tuple-element.12.vel_in, f32[2,12,128]{2,1,0:T(8,128)} %fusion.mask_in), custom_call_target="tpu_custom_call" | custom-call | tf_op jit(solution)/shard_map/verlet/pallas_call | solution.py:238
  148.0 0.0 copy-start.1
  148.0 1.4 copy.8
  149.5 0.0 copy-start
  149.5 0.0 copy-done.1
  149.5 0.6 copy.9
  150.1 0.2 copy-done
  150.3 0.6 copy.10
Async XLA Ops:
  0.6 0.7 copy-start.2
  148.0 1.5 copy-start.1
  149.5 0.8 copy-start

commit v3 on v2

--- a/solution.py
+++ b/solution.py
@@ -15,6 +15,7 @@
 
 FEATURES = 32
 TALL = 32
+LANES = (0, 2, 1)
 NEAR = (-1, 0, 1)
 MESH = pl.DeviceIdType.MESH
 
@@ -116,7 +117,7 @@
             put(near_rows, (u, v), 18 + place, FEATURES, value)
         for row, value in enumerate((spots[0], spots[1], spots[2] - 1.0, spots[2], spots[2] + 1.0)):
             put(frame, (u, v), row, 8, value)
-        near_cols[v, :, u * slots:(u + 1) * slots] = near_rows[u, v].astype(bf16)
+        near_cols[v, :, LANES[u] * slots:(LANES[u] + 1) * slots] = near_rows[u, v].astype(bf16)
 
     def build_own(column):
         v = column + 1
@@ -145,19 +146,33 @@
     def layers_of(z):
         return [lax.rem(z + r + depth, depth) for r in NEAR]
 
-    def first_pass(cell, carry):
-        column, z = lax.div(cell, depth), lax.rem(cell, depth)
+    def own_side(column, q):
+        return 1 <= column + q <= columns
+
+    def reaches(cell, column, z, density, groups):
         layers = layers_of(z)
-        density = jnp.zeros((slots, slots), f32)
         for r in range(3):
             start = pl.multiple_of(layers[r] * FEATURES, FEATURES)
-            for q in range(3):
-                near = near_cols[column + q, pl.ds(start, FEATURES), :]
+            for q, order in groups:
+                low, high = LANES[order[0]], LANES[order[-1]] + 1
+                near = near_cols[column + q, pl.ds(start, FEATURES), low * slots:high * slots]
                 reach = jnp.maximum(jnp.dot(self_cols[r, cell], near, preferred_element_type=f32), 0.0)
-                for u in range(3):
-                    part = reach[:, u * slots:(u + 1) * slots]
+                for place, u in enumerate(order):
+                    part = reach[:, place * slots:(place + 1) * slots]
                     held[cell, (q * 3 + r) * 3 + u] = part
                     density = density + part * part
+        return density
+
+    def first_own(column, z, carry):
+        cell = column * depth + z
+        groups = [(q, (1,)) for q in range(3) if own_side(column, q)]
+        own_slopes[cell] = reaches(cell, column, z, jnp.zeros((slots, slots), f32), groups)
+        return carry
+
+    def first_rest(column, z, carry):
+        cell = column * depth + z
+        groups = [(q, (0, 2) if own_side(column, q) else (0, 2, 1)) for q in range(3)]
+        density = reaches(cell, column, z, own_slopes[cell], groups)
         present = places[1, column + 1, 3, pl.ds(z, 1), :]
         density = DENSITY_SCALE * (jnp.sum(density.T, axis=0, keepdims=True) - present)
         slope = DENSITY_SCALE / (4.0 * PAIR_SCALE) / jnp.sqrt(1.0 + density)
@@ -165,50 +180,66 @@
         own_slopes[cell] = jnp.broadcast_to(slope, (slots, slots)).T
         return carry
 
-    def second_pass(cell, carry):
-        column, z = lax.div(cell, depth), lax.rem(cell, depth)
+    def pulls(cell, column, z, rows, sums, chosen):
         layers = layers_of(z)
+        own = own_slopes[cell, rows, :]
+        for q, u in chosen:
+            for r in range(3):
+                at = [frame[u, column + q, pl.ds(layers[r] * 8 + row, 1), :] for row in (0, 1, 2 + r, 5)]
+                reach = held[cell, (q * 3 + r) * 3 + u, rows, :]
+                pull = reach * ((own + at[3]) - reach * reach)
+                for c in range(3):
+                    sums[c] = sums[c] + pull * at[c]
+                sums[3] = sums[3] + pull
+        for c in range(4):
+            totals[cell, c, rows, :] = sums[c]
+
+    def second_own(column, z, carry):
+        chosen = [(q, 1) for q in range(3) if own_side(column, q)]
         for block in range(slots // TALL):
             rows = pl.ds(block * TALL, TALL)
-            own = own_slopes[cell, rows, :]
-            sums = [jnp.zeros((TALL, slots), f32)] * 4
-            for q in range(3):
-                for r in range(3):
-                    for u in range(3):
-                        at = [frame[u, column + q, pl.ds(layers[r] * 8 + row, 1), :] for row in (0, 1, 2 + r, 5)]
-                        reach = held[cell, (q * 3 + r) * 3 + u, rows, :]
-                        pull = reach * ((own + at[3]) - reach * reach)
-                        for c in range(3):
-                            sums[c] = sums[c] + pull * at[c]
-                        sums[3] = sums[3] + pull
-            for c in range(4):
-                totals[c, rows, :] = sums[c]
-        summed = [jnp.sum(totals[c].T, axis=0, keepdims=True) for c in range(4)]
+            pulls(column * depth + z, column, z, rows, [jnp.zeros((TALL, slots), f32)] * 4, chosen)
+        return carry
+
+    def second_rest(column, z, carry):
+        cell = column * depth + z
+        chosen = [(q, u) for q in range(3) for u in range(3) if u != 1 or not own_side(column, q)]
+        for block in range(slots // TALL):
+            rows = pl.ds(block * TALL, TALL)
+            pulls(cell, column, z, rows, [totals[cell, c, rows, :] for c in range(4)], chosen)
+        summed = [jnp.sum(totals[cell, c].T, axis=0, keepdims=True) for c in range(4)]
         for c, row in enumerate((0, 1, 3)):
             own = frame[1, column + 1, pl.ds(z * 8 + row, 1), :]
             partial[column, pl.ds(z * 8 + c, 1), :] = (8.0 * PAIR_SCALE) * (summed[c] - own * summed[3])
         return carry
 
+    def over_cells(body):
+        for column in range(columns):
+            lax.fori_loop(0, depth, functools.partial(body, column), 0)
+
+    halo = [(u, v) for u in range(3) for v in range(wide) if u != 1 or v in (0, wide - 1)]
+
     def evaluate(step, carry):
         copies = exchange(places, sizes, columns, place_send, place_recv)
         for column in range(columns):
             build_own(column)
             build_column(1, column + 1)
         lax.fori_loop(0, cells, turned, 0)
+        over_cells(first_own)
         for copy in copies:
             copy.wait()
-        for u in range(3):
-            for v in range(wide):
-                if u != 1 or v in (0, wide - 1):
-                    build_column(u, v)
-        lax.fori_loop(0, cells, first_pass, 0)
+        for u, v in halo:
+            build_column(u, v)
+        over_cells(first_rest)
         copies = exchange(slopes, sizes, columns, slope_send, slope_recv)
+        for v in range(1, columns + 1):
+            put(frame, (1, v), 5, 8, slopes[1, v])
+        over_cells(second_own)
         for copy in copies:
             copy.wait()
-        for u in range(3):
-            for v in range(wide):
-                put(frame, (u, v), 5, 8, slopes[u, v])
-        lax.fori_loop(0, cells, second_pass, 0)
+        for u, v in halo:
+            put(frame, (u, v), 5, 8, slopes[u, v])
+        over_cells(second_rest)
         begin = jnp.where(step > 0, 0.5 * TIME_STEP, 0.0)
         end = jnp.where(step < STEPS, 0.5 * TIME_STEP, 0.0)
         drift = jnp.where(step < STEPS, TIME_STEP, 0.0)
@@ -250,7 +281,7 @@
             pltpu.VMEM((3, cells, slots, FEATURES), bf16),
             pltpu.VMEM((cells, slots, slots), f32),
             pltpu.VMEM((cells, 27, slots, slots), f32),
-            pltpu.VMEM((4, slots, slots), f32),
+            pltpu.VMEM((cells, 4, slots, slots), f32),
             pltpu.VMEM((columns, depth * 8, slots), f32),
             pltpu.SemaphoreType.DMA((8,)),
             pltpu.SemaphoreType.DMA((8,)),

time: 151 us -> 140 us (0.927)
  Pallas kernels: 145 us -> 134 us
    pallas_call x1, Pallas kernels: 145 us -> 134 us  [shards(): pl.pallas_call(functools.partial(kernel, sizes, columns, depth, slots), o...]
where the time goes in v3:
time: 140 us
  Pallas kernels  134 us (96%)
  local copies, waits for them, and re-layouts  4.98 us (4%)
    pallas_call x1, Pallas kernels, shards(): pl.pallas_call(functools.partial(kernel, sizes, columns, depth, slots), o...  134 us
    unnamed x9, local copies, waits for them, and re-layouts  3.55 us

profile of v3, /device:TPU:0, one launch (start us, length us, event | category | flops | bytes accessed | tf_op | source)
XLA Modules:
  0.0 139.8 jit_solution(16148971744121146518)
XLA Ops:
  0.6 0.0 copy-start.2
  0.6 0.7 copy-done.2
  1.3 0.7 fusion.mask_in
  2.0 1.4 %copy_bitcast_fusion = (f32[3,2,12,128]{3,2,1,0:T(8,128)}, f32[3,2,12,128]{3,2,1,0:T(8,128)}) fusion(f32[3,1,2,12,128]{4,2,3,1,0:T(2,128)} %param.4, f32[3,1,2,12,128]{4,2,3,1,0:T(2,128)} %param.3), kind=kLoop, calls=%fused_computation | loop fusion | bytes 147456 | tf_op jit(solution)/shard_map/reshape | solution.py:295
  3.4 133.5 %verlet.1 = (f32[3,2,12,128]{3,2,1,0:T(8,128)}, f32[3,2,12,128]{3,2,1,0:T(8,128)}, f32[3,2,12,128]{3,2,1,0:T(8,128)}) custom-call(f32[3,2,12,128]{3,2,1,0:T(8,128)} %get-tuple-element.13.pos_in, f32[3,2,12,128]{3,2,1,0:T(8,128)} %get-tuple-element.12.vel_in, f32[2,12,128]{2,1,0:T(8,128)} %fusion.mask_in), custom_call_target="tpu_custom_call" | custom-call | tf_op jit(solution)/shard_map/verlet/pallas_call | solution.py:269
  136.9 0.0 copy-start.1
  136.9 1.4 %copy.8 = f32[3,1,2,12,128]{4,2,3,1,0:T(2,128)} copy(f32[3,1,2,12,128]{4,3,2,0,1:T(8,128)} %bitcast.10) | data formatting | bytes 73728
  138.4 0.0 copy-start
  138.4 0.0 copy-done.1
  138.4 0.6 copy.9
  139.0 0.2 copy-done
  139.2 0.6 copy.10
Async XLA Ops:
  0.6 0.7 copy-start.2
  136.9 1.5 %copy-start.1 = (f32[3,2,12,128]{3,2,1,0:T(8,128)S(1)}, f32[3,2,12,128]{3,2,1,0:T(8,128)}, u32[]{:S(2)}) copy-start(f32[3,2,12,128]{3,2,1,0:T(8,128)} %get-tuple-element.7) | copy-start | bytes 110596
  138.4 0.8 copy-start

commit v4 on v3

--- a/solution.py
+++ b/solution.py
@@ -14,7 +14,7 @@
 ABSENT = 1.0e6
 
 FEATURES = 32
-TALL = 32
+TALL = 64
 LANES = (0, 2, 1)
 NEAR = (-1, 0, 1)
 MESH = pl.DeviceIdType.MESH

time: 140 us -> 140 us (level)
  no operation moved by 1% of the time
where the time goes in v4:
time: 140 us
  Pallas kernels  134 us (96%)
  local copies, waits for them, and re-layouts  4.98 us (4%)
    pallas_call x1, Pallas kernels, shards(): pl.pallas_call(functools.partial(kernel, sizes, columns, depth, slots), o...  134 us
    unnamed x9, local copies, waits for them, and re-layouts  3.55 us

profile of v4, /device:TPU:0, one launch (start us, length us, event | category | flops | bytes accessed | tf_op | source)
XLA Modules:
  0.0 139.9 jit_solution(1432148861907807674)
XLA Ops:
  0.6 0.0 copy-start.2
  0.6 0.7 copy-done.2
  1.3 0.7 fusion.mask_in
  2.0 1.4 %copy_bitcast_fusion = (f32[3,2,12,128]{3,2,1,0:T(8,128)}, f32[3,2,12,128]{3,2,1,0:T(8,128)}) fusion(f32[3,1,2,12,128]{4,2,3,1,0:T(2,128)} %param.4, f32[3,1,2,12,128]{4,2,3,1,0:T(2,128)} %param.3), kind=kLoop, calls=%fused_computation | loop fusion | bytes 147456 | tf_op jit(solution)/shard_map/reshape | solution.py:295
  3.4 133.6 %verlet.1 = (f32[3,2,12,128]{3,2,1,0:T(8,128)}, f32[3,2,12,128]{3,2,1,0:T(8,128)}, f32[3,2,12,128]{3,2,1,0:T(8,128)}) custom-call(f32[3,2,12,128]{3,2,1,0:T(8,128)} %get-tuple-element.13.pos_in, f32[3,2,12,128]{3,2,1,0:T(8,128)} %get-tuple-element.12.vel_in, f32[2,12,128]{2,1,0:T(8,128)} %fusion.mask_in), custom_call_target="tpu_custom_call" | custom-call | tf_op jit(solution)/shard_map/verlet/pallas_call | solution.py:269
  137.0 0.0 copy-start.1
  137.0 1.4 %copy.8 = f32[3,1,2,12,128]{4,2,3,1,0:T(2,128)} copy(f32[3,1,2,12,128]{4,3,2,0,1:T(8,128)} %bitcast.10) | data formatting | bytes 73728
  138.5 0.0 copy-start
  138.5 0.0 copy-done.1
  138.5 0.6 copy.9
  139.1 0.2 copy-done
  139.3 0.6 copy.10
Async XLA Ops:
  0.6 0.7 copy-start.2
  137.0 1.5 %copy-start.1 = (f32[3,2,12,128]{3,2,1,0:T(8,128)S(1)}, f32[3,2,12,128]{3,2,1,0:T(8,128)}, u32[]{:S(2)}) copy-start(f32[3,2,12,128]{3,2,1,0:T(8,128)} %get-tuple-element.7) | copy-start | bytes 110596
  138.5 0.8 copy-start
